TPU v7x, 256 devices: a whole 4x4x8 slice. The times are simulated.
256 devices in a mesh: inner: 32 (over z_lo, y, core), outer: 8 (over x, z_hi).
Axes of the slice: x: 4, y: 4, z: 8 (z_hi: 2, z_lo: 4; z = z_hi * 4 + z_lo), core: 2. Of those that a mesh axis runs over, the one named last changes fastest.
Arguments:
- samples: float32 [2, 256, 262144], P(None, ('inner', 'outer')), may hold values from -6 to 6
- gram_index: int32 [8388608], P(('inner', 'outer')), may hold values from 0 to 7, as said below
- gram_offset: int32 [8388608], P(('inner', 'outer')), may hold values from 0 to 31
Outputs:
- z_field: float32 [67108864], P(('inner', 'outer'))
- gram_values: float32 [8388608], P(('inner', 'outer'))
Inputs may be any that keep to these rules, and one draw needn't show every extreme that they name: `gram_index`: A device's first Gram point has 0 and its last 7.
All inputs are finite; a program needn't handle non-finite values.
Results may differ from a plain program's by a relative error of at most 0.00007.
Values sent between devices are 32-bit elements; how exact they have to be, the bound alone decides.
No kernel may reach another device: no remote copies, remote signals or barrier semaphores. Data moves between devices by JAX's collectives and lax.ppermute only.
A program may use at most 256 MiB of HBM per device.

v0:
```python
import functools
import math

import jax
import jax.numpy as jnp
import numpy as np
from jax import lax
from jax.experimental import pallas as pl
from jax.experimental.pallas import tpu as pltpu
from jax.sharding import PartitionSpec as P

GAP = 8
HALF = 16
UPS = 32
RATE = 4.0
SPREAD = HALF / 2.0
SIDE = 512
LANES = 128
AXES = ("inner", "outer")
F32 = jnp.float32
BF16 = jnp.bfloat16
MIB = 1 << 20


def halves(table):
    high = table.astype(jnp.bfloat16)
    low = (table - high.astype(np.float64)).astype(jnp.bfloat16)
    return np.stack([high, low])


def segment_tables():
    sample = np.arange(LANES)
    tables = []
    for g in range(4):
        angle = 2.0 * np.pi * ((4 * sample[:, None] + g) * sample[None, :] % SIDE) / SIDE
        cos, sin = np.cos(angle), np.sin(angle)
        tables.append(np.block([[cos, sin], [-sin, cos]]))
    return halves(np.stack(tables))


def twiddle_table():
    u = np.arange(SIDE).reshape(LANES, 4).T.reshape(SIDE)
    c = np.arange(SIDE)
    angle = -2.0 * np.pi * (u[:, None] * c[None, :]) / (SIDE * SIDE)
    return np.stack([np.cos(angle), np.sin(angle)]).astype(np.float32)


def device_table(devices):
    n = np.arange(devices)
    angle = 2.0 * np.pi * (n[:, None] * n[None, :] % devices) / devices
    return halves(np.concatenate([np.cos(angle), np.sin(angle)], axis=1))


def split(x):
    high = x.astype(BF16)
    return high, (x - high.astype(F32)).astype(BF16)


def dot(a, b, dims):
    return lax.dot_general(a, b, (dims, ((), ())), preferred_element_type=F32)


def dot3(a, b, dims=((1,), (0,))):
    (a_high, a_low), (b_high, b_low) = a, b
    return dot(a_high, b_high, dims) + (dot(a_high, b_low, dims) + dot(a_low, b_high, dims))


def quarter(parts):
    (r0, i0), (r1, i1), (r2, i2), (r3, i3) = parts
    ar, ai, br, bi = r0 + r2, i0 + i2, r0 - r2, i0 - i2
    cr, ci, er, ei = r1 + r3, i1 + i3, r1 - r3, i1 - i3
    return [(ar + cr, ai + ci), (br + ei, bi - er), (ar - cr, ai - ci), (br - ei, bi + er)]


def times(a, b):
    return a[0] * b[0] - a[1] * b[1], a[0] * b[1] + a[1] * b[0]


def segment_kernel(devices, place_ref, x_ref, table_ref, twiddle_ref, out_ref, first_ref, second_ref):
    place = place_ref[0]
    length = SIDE * SIDE * devices
    for j in range(4):
        grid = [
            tuple(x_ref[part, pl.ds(SIDE * i + j, LANES, stride=4), :] for part in range(2))
            for i in range(4)
        ]
        for g, pair in enumerate(quarter(grid)):
            for part in range(2):
                high, low = split(pair[part])
                rows, cols = pl.ds(LANES * part, LANES), pl.ds(LANES * j, LANES)
                first_ref[0, g, rows, cols] = high
                first_ref[1, g, rows, cols] = low
    for g in range(4):
        done = dot3((table_ref[0, g], table_ref[1, g]), (first_ref[0, g], first_ref[1, g]))
        u = 4 * lax.broadcasted_iota(jnp.int32, (LANES, LANES), 0) + g
        angle = (place * u).astype(F32) * (-2.0 * math.pi / length)
        square = angle * angle
        turn = (
            1.0 - square * (0.5 - square * (1.0 / 24.0)),
            angle * (1.0 - square * (1.0 / 6.0 - square * (1.0 / 120.0))),
        )
        rows = pl.ds(LANES * g, LANES)
        grid = []
        for j in range(4):
            cols = slice(LANES * j, LANES * (j + 1))
            both = times((twiddle_ref[0, rows, cols], twiddle_ref[1, rows, cols]), turn)
            grid.append(times((done[:LANES, cols], done[LANES:, cols]), both))
        for h, pair in enumerate(quarter(grid)):
            for part in range(2):
                high, low = split(pair[part])
                cols = pl.ds(LANES * part, LANES)
                second_ref[0, h, rows, cols] = high
                second_ref[1, h, rows, cols] = low
    for h in range(4):
        done = dot3(
            (second_ref[0, h], second_ref[1, h]), (table_ref[0, h], table_ref[1, h]), ((1,), (1,))
        )
        v = 4 * lax.broadcasted_iota(jnp.int32, (8, LANES), 1) + h
        angle = (place * v).astype(F32) * (-2.0 * math.pi * SIDE / length)
        turn = (jnp.cos(angle)[:1], jnp.sin(angle)[:1])
        pair = times((done[:, :LANES], done[:, LANES:]), turn)
        for part in range(2):
            for upper in range(2):
                out_ref[pl.ds(8 * part + 4 * upper + h, SIDE // 2, stride=16), :] = pair[part][
                    SIDE // 2 * upper : SIDE // 2 * (upper + 1)
                ]


def device_kernel(devices, x_ref, table_ref, out_ref):
    for block in range(4):
        columns = []
        for e in (2 * block, 2 * block + 1):
            columns.append(
                jnp.concatenate(
                    [x_ref[pl.ds(8 * part + e, devices, stride=16), :] for part in range(2)], axis=0
                )
            )
        x = jnp.concatenate(columns, axis=1)
        done = dot3((table_ref[0], table_ref[1]), split(x))
        for i, e in enumerate((2 * block, 2 * block + 1)):
            out_ref[pl.ds(e, devices, stride=8), :] = done[:, LANES * i : LANES * (i + 1)]


def gain(devices, place, position):
    length = SIDE * SIDE * devices
    centred = place.astype(F32) / devices + position.astype(F32) / length - 0.5
    return length ** (-0.5) * jnp.exp(RATE * centred * centred)


def gram_kernel(devices, place_ref, x_ref, index_ref, offset_ref, z_ref, gram_ref, zs, ids, offs, sums):
    place = place_ref[0]
    pad = HALF
    t = lax.broadcasted_iota(jnp.int32, (LANES, LANES), 0)
    lane = lax.broadcasted_iota(jnp.int32, (LANES, LANES), 1)
    for h in range(4):
        for g in range(4):
            start = 8 * LANES * (g % 2) + 4 * (g // 2) + h
            raw = x_ref[pl.ds(start, LANES, stride=8), :]
            position = SIDE * (4 * lane + h) + 4 * t + g
            zs[h, pl.ds(pad + g, LANES, stride=4), :] = raw * gain(devices, place, position)
        for block in range(4):
            z_ref[pl.ds(4 * h + block, LANES, stride=16), :] = zs[
                h, pl.ds(pad + LANES * block, LANES), :
            ].T
    edge = lane[:pad]
    for h in range(4):
        before = zs[(h - 1) % 4, pl.ds(SIDE, pad), :]
        after = zs[(h + 1) % 4, pl.ds(pad, pad), :]
        if h == 0:
            before = jnp.where(edge == 0, 0.0, pltpu.roll(before, 1, 1))
        if h == 3:
            after = jnp.where(edge == LANES - 1, 0.0, pltpu.roll(after, LANES - 1, 1))
        zs[h, pl.ds(0, pad), :] = before
        zs[h, pl.ds(pad + SIDE, pad), :] = after
    for odd in range(2):
        ids[odd] = index_ref[pl.ds(odd, LANES, stride=2), :].T
        offs[odd] = offset_ref[pl.ds(odd, LANES, stride=2), :].T
    for h in range(4):

        def body(step, carry, h=h):
            rows = pl.ds(pl.multiple_of(64 * (h % 2) + 8 * step, 8), 8)
            index = ids[h // 2, rows, :]
            fraction = offs[h // 2, rows, :].astype(F32) * (1.0 / UPS)
            taps = [
                zs[h, pl.ds(pad + o + 64 * step, 8, stride=8), :]
                for o in range(1 - HALF, HALF + GAP)
            ]
            for bit in (2, 1, 0):
                size = 1 << bit
                chosen = (index >> bit & 1) == 1
                taps = [jnp.where(chosen, b, a) for a, b in zip(taps[:-size], taps[size:])]
            sums[h // 2, rows, :] = weighted(taps, fraction)
            return carry

        lax.fori_loop(0, 8, body, 0)
    for odd in range(2):
        gram_ref[pl.ds(odd, LANES, stride=2), :] = sums[odd].T


def weighted(taps, fraction):
    near = jnp.exp(fraction * fraction * (-0.5 / (SPREAD * SPREAD)))
    sine = jnp.sin(math.pi * fraction) * (near / math.pi)
    up = jnp.exp(fraction * (1.0 / (SPREAD * SPREAD)))
    down = jnp.exp(fraction * (-1.0 / (SPREAD * SPREAD)))
    square = fraction * fraction
    ups, downs = up, down
    total = None
    for w in range(1, HALF + 1):
        scale = (-1.0) ** w * math.exp(-0.5 * w * w / (SPREAD * SPREAD))
        term = (ups * taps[HALF - 1 + w]) * (fraction + w)
        if w < HALF:
            term = term + (downs * taps[HALF - 1 - w]) * (fraction - w)
        term = term * (scale / (square - w * w))
        total = term if total is None else total + term
        ups, downs = ups * up, downs * down
    at_zero = fraction == 0.0
    middle = jnp.where(at_zero, 1.0, sine / jnp.where(at_zero, 1.0, fraction))
    return sine * total + middle * taps[HALF - 1]


def weight(distance):
    at_zero = distance == 0.0
    safe = jnp.where(at_zero, 1.0, distance)
    sinc = jnp.where(at_zero, 1.0, jnp.sin(math.pi * safe) / (math.pi * safe))
    return sinc * jnp.exp(-0.5 * distance * distance / (SPREAD * SPREAD))


def call(kernel, out_shape, smem, count, scratch=(), flops=0, out_count=1):
    vmem = pl.BlockSpec(memory_space=pltpu.VMEM)
    first = [pl.BlockSpec(memory_space=pltpu.SMEM)] * smem
    return pl.pallas_call(
        kernel,
        out_shape=out_shape,
        in_specs=first + [vmem] * count,
        out_specs=vmem if out_count == 1 else (vmem,) * out_count,
        scratch_shapes=list(scratch),
        compiler_params=pltpu.CompilerParams(vmem_limit_bytes=48 * MIB),
        cost_estimate=pl.CostEstimate(flops=flops, bytes_accessed=4 * MIB, transcendentals=0),
    )


def segment_transform(devices, place, samples):
    points = samples.size // 2
    return call(
        functools.partial(segment_kernel, devices),
        jax.ShapeDtypeStruct((points * 2 // LANES, LANES), F32),
        1,
        3,
        [pltpu.VMEM((2, 4, 2 * LANES, SIDE), BF16), pltpu.VMEM((2, 4, SIDE, 2 * LANES), BF16)],
        3 * 2 * 8 * SIDE * SIDE * LANES,
    )(place, samples, jnp.asarray(segment_tables()), jnp.asarray(twiddle_table()))


def device_transform(devices, received):
    return call(
        functools.partial(device_kernel, devices),
        jax.ShapeDtypeStruct((received.shape[0] // 2, LANES), F32),
        0,
        2,
        (),
        3 * 2 * 2 * devices * received.shape[0] // 2 * LANES,
    )(received, jnp.asarray(device_table(devices)))


def interpolate(devices, place, timed, index, offset):
    return call(
        functools.partial(gram_kernel, devices),
        (jax.ShapeDtypeStruct(timed.shape, F32), jax.ShapeDtypeStruct(index.shape, F32)),
        1,
        3,
        [
            pltpu.VMEM((4, SIDE + 2 * HALF, LANES), F32),
            pltpu.VMEM((2, LANES, LANES), jnp.int32),
            pltpu.VMEM((2, LANES, LANES), jnp.int32),
            pltpu.VMEM((2, LANES, LANES), F32),
        ],
        1 << 26,
        2,
    )(place, timed, index, offset)


def ends(devices, place, timed):
    grid = timed.reshape(2, LANES, 2, 4, LANES)
    count = HALF // 4
    first = jnp.transpose(grid[:, :count, :, 0, 0], (1, 2, 0)).reshape(HALF)
    last = jnp.transpose(grid[:, LANES - count :, :, 3, LANES - 1], (1, 2, 0)).reshape(HALF)
    spot = jnp.arange(HALF, dtype=jnp.int32)
    return (
        first * gain(devices, place, spot),
        last * gain(devices, place, spot + SIDE * SIDE - HALF),
    )


def from_ends(before, after, index, offset):
    points = 2
    count = index.shape[0]
    spot = jnp.arange(HALF, dtype=jnp.int32)[None, :]
    j = jnp.arange(points, dtype=jnp.int32)

    def part(halo, ids, anchor, place):
        tap = place - (anchor + index[ids])[:, None]
        held = (tap > -HALF) & (tap <= HALF)
        distance = (offset[ids].astype(F32) / UPS)[:, None] - tap.astype(F32)
        return jnp.sum(jnp.where(held, halo[None, :] * weight(distance), 0.0), axis=1)

    head = part(before, slice(0, points), GAP * j, spot - HALF)
    tail = part(
        after, slice(count - points, count), GAP * (j + count - points), spot + GAP * count
    )
    return head, tail


def local(samples, gram_index, gram_offset):
    inner, outer = lax.axis_size("inner"), lax.axis_size("outer")
    devices = inner * outer
    place = (lax.axis_index("inner") * outer + lax.axis_index("outer")).astype(jnp.int32)
    spot = place.reshape(1)
    points = samples.shape[2]
    parts = segment_transform(devices, spot, samples.reshape(2, points // LANES, LANES))
    received = lax.all_to_all(parts.reshape(devices, 16, LANES), AXES, 0, 0, tiled=True)
    real = device_transform(devices, received.reshape(16 * devices, LANES))
    timed = lax.all_to_all(real.reshape(devices, 8, LANES), AXES, 0, 0, tiled=True)
    timed = timed.reshape(8 * devices, LANES)
    first, last = ends(devices, place, timed)
    up = [(i, i + 1) for i in range(devices - 1)]
    before = lax.ppermute(last, AXES, up)
    after = lax.ppermute(first, AXES, [(j, i) for i, j in up])
    rows = gram_index.shape[0] // LANES
    z_field, gram = interpolate(
        devices, spot, timed, gram_index.reshape(rows, LANES), gram_offset.reshape(rows, LANES)
    )
    gram = gram.reshape(-1)
    head, tail = from_ends(before, after, gram_index, gram_offset)
    gram = gram.at[: head.shape[0]].add(head).at[gram.shape[0] - tail.shape[0] :].add(tail)
    return z_field.reshape(points), gram


def solution(mesh):
    return jax.shard_map(
        local,
        mesh=mesh,
        in_specs=(P(None, AXES, None), P(AXES), P(AXES)),
        out_specs=(P(AXES), P(AXES)),
        check_vma=False,
    )
```

profile of v0, /device:TPU:1, one launch (start us, length us, event | category | flops | bytes accessed | tf_op | source)
XLA Modules:
  0.0 137.3 jit_solution(18011753291321217332)
XLA Ops:
  0.6 0.0 copy-start
  0.6 1.6 %copy-done = f32[2,1,262144]{2,1,0:T(1,128)S(1)} copy-done((f32[2,1,262144]{2,1,0:T(1,128)S(1)}, f32[2,1,262144]{2,1,0:T(1,128)}, u32[]{:S(2)}) %copy-start) | copy-done | bytes 2097176
  2.2 0.0 copy-start.1
  2.2 1.2 copy-done.1
  3.5 4.9 %shard_map.77 = f32[4096,128]{1,0:T(8,128)S(1)} custom-call(s32[1]{0:T(128)} %bitcast.place_ref, f32[2,2048,128]{2,1,0:T(8,128)S(1)} %bitcast.20, bf16[2,4,256,256]{3,2,1,0:T(8,128)(2,1)S(1)} %copy-done.1, f32[2,512,512]{2,1,0:T(8,128)} %constant.114.clone.twiddle_ref), custom_call_target="tpu_custom_call" | custom-call | flops 1610612736 | bytes 4194304 | tf_op jit(solution)/shard_map/pallas_call | solution.py:244
  8.3 0.0 copy-start.2
  8.3 67.8 %all_to_all.10 = f32[256,16,128]{2,1,0:T(8,128)S(1)} all-to-all(f32[256,16,128]{2,1,0:T(8,128)S(1)} %bitcast.19), channel_id=1, replica_groups=mesh['inner'=32,'outer'=8] {'inner','outer'}, dimensions={0} | all-to-all | bytes 4194304 | tf_op jit(solution)/shard_map/all_to_all | solution.py:320
  76.1 0.0 copy-done.2
  76.1 0.0 copy-start.3
  76.1 0.0 copy-start.4
  76.1 2.5 %shard_map.78 = f32[2048,128]{1,0:T(8,128)} custom-call(f32[4096,128]{1,0:T(8,128)S(1)} %bitcast.18, bf16[2,256,512]{2,1,0:T(8,128)(2,1)S(1)} %copy-done.2), custom_call_target="tpu_custom_call" | custom-call | flops 805306368 | bytes 4194304 | tf_op jit(solution)/shard_map/pallas_call | solution.py:255
  78.6 7.3 %all-to-all-start.1 = ((f32[256,8,128]{2,1,0:T(8,128)}), f32[256,8,128]{2,1,0:T(8,128)S(1)}, u32[]{:S(2)}, u32[]{:S(2)}) async-start(f32[256,8,128]{2,1,0:T(8,128)} %bitcast.4), calls=%async_computation.1 | async-start | bytes 2097152 | tf_op jit(solution)/shard_map/all_to_all | solution.py:322
  85.9 0.0 copy-done.3
  85.9 0.1 slice_add_fusion.2
  86.0 0.0 copy-done.4
  86.0 0.1 convert_multiply_fusion
  86.1 30.9 %all-to-all-done.1 = f32[256,8,128]{2,1,0:T(8,128)S(1)} async-done(((f32[256,8,128]{2,1,0:T(8,128)}), f32[256,8,128]{2,1,0:T(8,128)S(1)}, u32[]{:S(2)}, u32[]{:S(2)}) %all-to-all-start.1) | async-done | bytes 1048608 | tf_op jit(solution)/shard_map/all_to_all | solution.py:322
  117.0 0.2 copy.21
  117.2 0.1 fusion.22
  117.3 0.1 copy.26
  117.4 0.1 reshape.107
  117.5 3.8 %collective-permute-start = (f32[16]{0:T(128)S(1)}, f32[16]{0:T(128)S(1)}, u32[]{:S(2)}, u32[]{:S(2)}) collective-permute-start(f32[16]{0:T(128)S(1)} %fusion.16), channel_id=1, source_target_pairs={{0,1},{1,2},{2,3},{3,4},{4,5},{5,6},{6,7},{7,8},{8,9},{9,10},{10,1... | collective-permute-start | bytes 200 | tf_op jit(solution)/shard_map/ppermute | solution.py:326
  121.4 0.1 copy.27
  121.5 0.1 reshape.108
  121.6 7.8 %collective-permute-start.1 = (f32[16]{0:T(128)S(1)}, f32[16]{0:T(128)S(1)}, u32[]{:S(2)}, u32[]{:S(2)}) collective-permute-start(f32[16]{0:T(128)S(1)} %fusion.19), channel_id=1, source_target_pairs={{1,0},{2,1},{3,2},{4,3},{5,4},{6,5},{7,6},{8,7},{9,8},{10,9},{11,1... | collective-permute-start | bytes 200 | tf_op jit(solution)/shard_map/ppermute | solution.py:327
  129.4 4.6 %shard_map.79 = (f32[2048,128]{1,0:T(8,128)}, f32[256,128]{1,0:T(8,128)}) custom-call(s32[1]{0:T(128)} %bitcast.place_ref, f32[2048,128]{1,0:T(8,128)S(1)} %bitcast.17, s32[256,128]{1,0:T(8,128)S(1)} %bitcast.21, s32[256,128]{1,0:T(8,128)S(1)} %bitcast.22), custom_call_target="tpu_custom_call" | custom-call | flops 67108864 | bytes 4194304 | tf_op jit(solution)/shard_map/pallas_call | solution.py:266
  134.0 0.0 collective-permute-done
  134.0 0.2 fusion.6
  134.2 1.4 %fusion.21 = f32[32768]{0:T(1024)} fusion(f32[32768]{0:T(1024)} %bitcast.27, f32[2]{0:T(128)S(1)} %fusion.6), kind=kLoop, calls=%fused_computation.37 | loop fusion | flops 2 | bytes 1032 | tf_op jit(solution)/shard_map/scatter-add | solution.py:334
  135.6 0.0 collective-permute-done.1
  135.6 0.2 fusion.13
  135.8 1.5 %fusion.20 = f32[32768]{0:T(1024)} fusion(f32[32768]{0:T(1024)} %fusion.21, f32[2]{0:T(128)S(1)} %fusion.13), kind=kLoop, calls=%fused_computation.35 | loop fusion | flops 2 | bytes 1032 | tf_op jit(solution)/shard_map/scatter-add | solution.py:334
  (4 shorter events, 0.0 us)
Async XLA Ops:
  0.6 1.6 %copy-start = (f32[2,1,262144]{2,1,0:T(1,128)S(1)}, f32[2,1,262144]{2,1,0:T(1,128)}, u32[]{:S(2)}) copy-start(f32[2,1,262144]{2,1,0:T(1,128)} %param.10) | copy-start | bytes 6291460
  2.2 1.2 copy-start.1
  8.3 67.8 %copy-start.2 = (bf16[2,256,512]{2,1,0:T(8,128)(2,1)S(1)}, bf16[2,256,512]{2,1,0:T(8,128)(2,1)}, u32[]{:S(2)}) copy-start(bf16[2,256,512]{2,1,0:T(8,128)(2,1)} %constant.115.clone.table_ref) | copy-start | bytes 1572868
  76.1 9.8 %copy-start.3 = (s32[32768]{0:T(1024)S(1)}, s32[32768]{0:T(1024)}, u32[]{:S(2)}) copy-start(s32[32768]{0:T(1024)} %param.11) | copy-start | bytes 393220
  76.1 9.9 %copy-start.4 = (s32[32768]{0:T(1024)S(1)}, s32[32768]{0:T(1024)}, u32[]{:S(2)}) copy-start(s32[32768]{0:T(1024)} %param.12) | copy-start | bytes 393220
  78.6 38.4 %all-to-all-start.1 = ((f32[256,8,128]{2,1,0:T(8,128)}), f32[256,8,128]{2,1,0:T(8,128)S(1)}, u32[]{:S(2)}, u32[]{:S(2)}) async-start(f32[256,8,128]{2,1,0:T(8,128)} %bitcast.4), calls=%async_computation.1 | async-start | bytes 2097152 | tf_op jit(solution)/shard_map/all_to_all | solution.py:322
  117.5 16.5 %collective-permute-start = (f32[16]{0:T(128)S(1)}, f32[16]{0:T(128)S(1)}, u32[]{:S(2)}, u32[]{:S(2)}) collective-permute-start(f32[16]{0:T(128)S(1)} %fusion.16), channel_id=1, source_target_pairs={{0,1},{1,2},{2,3},{3,4},{4,5},{5,6},{6,7},{7,8},{8,9},{9,10},{10,1... | collective-permute-start | bytes 200 | tf_op jit(solution)/shard_map/ppermute | solution.py:326
  121.6 14.0 %collective-permute-start.1 = (f32[16]{0:T(128)S(1)}, f32[16]{0:T(128)S(1)}, u32[]{:S(2)}, u32[]{:S(2)}) collective-permute-start(f32[16]{0:T(128)S(1)} %fusion.19), channel_id=1, source_target_pairs={{1,0},{2,1},{3,2},{4,3},{5,4},{6,5},{7,6},{8,7},{9,8},{10,9},{11,1... | collective-permute-start | bytes 200 | tf_op jit(solution)/shard_map/ppermute | solution.py:327
where the time goes:
time: 138 us; the launch traced here: 137 us
  blocking collectives  67.8 us (49%)
  waiting for transfers between devices  30.9 us (22%)
  starting transfers between devices  18.8 us (14%)
  Pallas kernels  11.9 us (9%)
  local copies, waits for them, and re-layouts  3.55 us (3%)
  other arithmetic  3.53 us (3%)
    all_to_all x1, blocking collectives, local(): lax.all_to_all(parts.reshape(devices, 16, LANES), AXES, 0, 0, tiled=True)  67.8 us
    all_to_all x1, waiting for transfers between devices, local(): lax.all_to_all(real.reshape(devices, 8, LANES), AXES, 0, 0, tiled=True)  30.9 us
    ppermute x1, starting transfers between devices, local(): after = lax.ppermute(first, AXES, [(j, i) for i, j in up])  7.76 us
    all_to_all x1, starting transfers between devices, local(): lax.all_to_all(real.reshape(devices, 8, LANES), AXES, 0, 0, tiled=True)  7.26 us
    pallas_call x1, Pallas kernels, segment_transform(): call(functools.partial(segment_kernel, devices), jax.ShapeDtypeStruct((po...  4.85 us
    pallas_call x1, Pallas kernels, interpolate(): call(functools.partial(gram_kernel, devices), (jax.ShapeDtypeStruct(timed...  4.63 us
    ppermute x1, starting transfers between devices, local(): before = lax.ppermute(last, AXES, up)  3.81 us
    scatter-add x2, other arithmetic, local(): gram.at[:head.shape[0]].add(head).at[gram.shape[0] - tail.shape[0]:]  2.88 us
  transfers between devices with their start and end apart: 3, of which 1 were waited for; matrix products, arithmetic and copies ran while one was open for 1% of the time, Pallas kernels for 3%

commit v1 on v0

v1 whole, which is shorter than its diff:
```python
import functools
import math

import jax
import jax.numpy as jnp
import numpy as np
from jax import lax
from jax.experimental import pallas as pl
from jax.experimental.pallas import tpu as pltpu
from jax.sharding import PartitionSpec as P

GAP = 8
HALF = 16
UPS = 32
RATE = 4.0
SPREAD = HALF / 2.0
SIDE = 512
LANES = 128
AXES = ("inner", "outer")
F32 = jnp.float32
BF16 = jnp.bfloat16
MIB = 1 << 20


def halves(table):
    high = table.astype(jnp.bfloat16)
    low = (table - high.astype(np.float64)).astype(jnp.bfloat16)
    return np.stack([high, low])


def segment_tables():
    sample = np.arange(LANES)
    tables = []
    for g in range(4):
        angle = 2.0 * np.pi * ((4 * sample[:, None] + g) * sample[None, :] % SIDE) / SIDE
        cos, sin = np.cos(angle), np.sin(angle)
        tables.append(np.block([[cos, sin], [-sin, cos]]))
    return halves(np.stack(tables))


def twiddle_table():
    u = np.arange(SIDE).reshape(LANES, 4).T.reshape(SIDE)
    c = np.arange(SIDE)
    angle = -2.0 * np.pi * (u[:, None] * c[None, :]) / (SIDE * SIDE)
    return np.stack([np.cos(angle), np.sin(angle)]).astype(np.float32)


def device_table(devices):
    n = np.arange(devices)
    angle = 2.0 * np.pi * (n[:, None] * n[None, :] % devices) / devices
    return halves(np.concatenate([np.cos(angle), np.sin(angle)], axis=1))


def split(x):
    high = x.astype(BF16)
    return high, (x - high.astype(F32)).astype(BF16)


def dot(a, b, dims):
    return lax.dot_general(a, b, (dims, ((), ())), preferred_element_type=F32)


def dot3(a, b, dims=((1,), (0,))):
    (a_high, a_low), (b_high, b_low) = a, b
    return dot(a_high, b_high, dims) + (dot(a_high, b_low, dims) + dot(a_low, b_high, dims))


def quarter(parts):
    (r0, i0), (r1, i1), (r2, i2), (r3, i3) = parts
    ar, ai, br, bi = r0 + r2, i0 + i2, r0 - r2, i0 - i2
    cr, ci, er, ei = r1 + r3, i1 + i3, r1 - r3, i1 - i3
    return [(ar + cr, ai + ci), (br + ei, bi - er), (ar - cr, ai - ci), (br - ei, bi + er)]


def times(a, b):
    return a[0] * b[0] - a[1] * b[1], a[0] * b[1] + a[1] * b[0]


def segment_kernel(
    devices, place_ref, x_hbm, table_hbm, twiddle_hbm, out_ref,
    x_ref, table_ref, twiddle_ref, first_ref, second_ref, sems,
):
    place = place_ref[0]
    length = SIDE * SIDE * devices
    loads = []
    for part in range(2):
        for i in range(4):
            rows = pl.ds(SIDE * i, SIDE)
            loads.append((x_hbm.at[part, rows], x_ref.at[part, rows]))
    loads.append((table_hbm, table_ref))
    for g in range(4):
        rows = pl.ds(LANES * g, LANES)
        loads.append((twiddle_hbm.at[:, rows], twiddle_ref.at[:, rows]))
    copies = [
        pltpu.make_async_copy(source, target, sems.at[k]) for k, (source, target) in enumerate(loads)
    ]
    for copy in copies:
        copy.start()
    for copy in copies[:8]:
        copy.wait()
    for j in range(4):
        grid = [
            tuple(x_ref[part, pl.ds(SIDE * i + j, LANES, stride=4), :] for part in range(2))
            for i in range(4)
        ]
        for g, pair in enumerate(quarter(grid)):
            for part in range(2):
                high, low = split(pair[part])
                rows, cols = pl.ds(LANES * part, LANES), pl.ds(LANES * j, LANES)
                first_ref[0, g, rows, cols] = high
                first_ref[1, g, rows, cols] = low
    copies[8].wait()
    for g in range(4):
        done = dot3((table_ref[0, g], table_ref[1, g]), (first_ref[0, g], first_ref[1, g]))
        u = 4 * lax.broadcasted_iota(jnp.int32, (LANES, LANES), 0) + g
        angle = (place * u).astype(F32) * (-2.0 * math.pi / length)
        square = angle * angle
        turn = (
            1.0 - square * (0.5 - square * (1.0 / 24.0)),
            angle * (1.0 - square * (1.0 / 6.0 - square * (1.0 / 120.0))),
        )
        rows = pl.ds(LANES * g, LANES)
        grid = []
        copies[9 + g].wait()
        for j in range(4):
            cols = slice(LANES * j, LANES * (j + 1))
            both = times((twiddle_ref[0, rows, cols], twiddle_ref[1, rows, cols]), turn)
            grid.append(times((done[:LANES, cols], done[LANES:, cols]), both))
        for h, pair in enumerate(quarter(grid)):
            for part in range(2):
                high, low = split(pair[part])
                cols = pl.ds(LANES * part, LANES)
                second_ref[0, h, rows, cols] = high
                second_ref[1, h, rows, cols] = low
    for h in range(4):
        done = dot3(
            (second_ref[0, h], second_ref[1, h]), (table_ref[0, h], table_ref[1, h]), ((1,), (1,))
        )
        v = 4 * lax.broadcasted_iota(jnp.int32, (8, LANES), 1) + h
        angle = (place * v).astype(F32) * (-2.0 * math.pi * SIDE / length)
        turn = (jnp.cos(angle)[:1], jnp.sin(angle)[:1])
        pair = times((done[:, :LANES], done[:, LANES:]), turn)
        for part in range(2):
            for upper in range(2):
                out_ref[pl.ds(8 * part + 4 * upper + h, SIDE // 2, stride=16), :] = pair[part][
                    SIDE // 2 * upper : SIDE // 2 * (upper + 1)
                ]


def device_kernel(devices, x_ref, table_ref, out_ref):
    for block in range(4):
        columns = []
        for e in (2 * block, 2 * block + 1):
            columns.append(
                jnp.concatenate(
                    [x_ref[pl.ds(8 * part + e, devices, stride=16), :] for part in range(2)], axis=0
                )
            )
        x = jnp.concatenate(columns, axis=1)
        done = dot3((table_ref[0], table_ref[1]), split(x))
        for i, e in enumerate((2 * block, 2 * block + 1)):
            out_ref[pl.ds(e, devices, stride=8), :] = done[:, LANES * i : LANES * (i + 1)]


def gain(devices, place, position):
    length = SIDE * SIDE * devices
    centred = place.astype(F32) / devices + position.astype(F32) / length - 0.5
    return length ** (-0.5) * jnp.exp(RATE * centred * centred)


def gram_tables_kernel(devices, place_ref, index_ref, offset_ref, gain_ref, ids_ref, weights_ref):
    place = place_ref[0]
    t = lax.broadcasted_iota(jnp.int32, (LANES, LANES), 0)
    lane = lax.broadcasted_iota(jnp.int32, (LANES, LANES), 1)
    for h in range(4):
        for g in range(4):
            position = SIDE * (4 * lane + h) + 4 * t + g
            gain_ref[h, g] = gain(devices, place, position)
    for odd in range(2):
        ids_ref[odd] = index_ref[pl.ds(odd, LANES, stride=2), :].T
        fraction = offset_ref[pl.ds(odd, LANES, stride=2), :].T.astype(F32) * (1.0 / UPS)
        put_weights(weights_ref, odd, fraction)


def put_weights(weights_ref, odd, fraction):
    near = jnp.exp(fraction * fraction * (-0.5 / (SPREAD * SPREAD)))
    sine = jnp.sin(math.pi * fraction) * (near / math.pi)
    up = jnp.exp(fraction * (1.0 / (SPREAD * SPREAD)))
    down = jnp.exp(fraction * (-1.0 / (SPREAD * SPREAD)))
    square = fraction * fraction
    ups, downs = sine * up, sine * down
    for w in range(1, HALF + 1):
        scale = (-1.0) ** w * math.exp(-0.5 * w * w / (SPREAD * SPREAD))
        share = scale / (square - w * w)
        weights_ref[HALF - 1 + w, odd] = ups * ((fraction + w) * share)
        if w < HALF:
            weights_ref[HALF - 1 - w, odd] = downs * ((fraction - w) * share)
        ups, downs = ups * up, downs * down
    at_zero = fraction == 0.0
    weights_ref[HALF - 1, odd] = jnp.where(at_zero, 1.0, sine / jnp.where(at_zero, 1.0, fraction))


def ends_kernel(x_ref, gain_ref, first_ref, last_ref):
    count = HALF // 4
    for g in range(4):
        for h, t, out_ref in ((0, 0, first_ref), (3, LANES - count, last_ref)):
            start = 8 * LANES * (g % 2) + 4 * (g // 2) + h
            low = t - t % 8
            raw = x_ref[pl.ds(start + 8 * low, 8, stride=8), :] * gain_ref[h, g, pl.ds(low, 8), :]
            out_ref[pl.ds(g, count, stride=4), :] = raw[t - low : t - low + count]


def times_kernel(x_ref, gain_ref, z_ref, held_ref):
    for h in range(4):
        for g in range(4):
            start = 8 * LANES * (g % 2) + 4 * (g // 2) + h
            raw = x_ref[pl.ds(start, LANES, stride=8), :]
            held_ref[h, pl.ds(g, LANES, stride=4), :] = raw * gain_ref[h, g]
        for block in range(4):
            z_ref[pl.ds(4 * h + block, LANES, stride=16), :] = held_ref[
                h, pl.ds(LANES * block, LANES), :
            ].T


def gram_kernel(before_ref, after_ref, held_ref, ids_ref, weights_ref, gram_ref, zs_ref, sums):
    pad = HALF
    edge = lax.broadcasted_iota(jnp.int32, (pad, LANES), 1)
    for h in range(4):
        before = held_ref[(h - 1) % 4, pl.ds(SIDE - pad, pad), :]
        after = held_ref[(h + 1) % 4, pl.ds(0, pad), :]
        if h == 0:
            before = jnp.where(edge == 0, pltpu.roll(before_ref[...], 1, 1), pltpu.roll(before, 1, 1))
        if h == 3:
            after = jnp.where(
                edge == LANES - 1,
                pltpu.roll(after_ref[...], LANES - 1, 1),
                pltpu.roll(after, LANES - 1, 1),
            )
        zs_ref[h, pl.ds(0, pad), :] = before
        zs_ref[h, pl.ds(pad, SIDE), :] = held_ref[h]
        zs_ref[h, pl.ds(pad + SIDE, pad), :] = after
    for h in range(4):

        def body(step, carry, h=h):
            rows = pl.ds(pl.multiple_of(64 * (h % 2) + 8 * step, 8), 8)
            index = ids_ref[h // 2, rows, :]
            taps = [
                zs_ref[h, pl.ds(pad + o + 64 * step, 8, stride=8), :]
                for o in range(1 - HALF, HALF + GAP)
            ]
            for bit in (2, 1, 0):
                size = 1 << bit
                chosen = (index >> bit & 1) == 1
                taps = [jnp.where(chosen, b, a) for a, b in zip(taps[:-size], taps[size:])]
            terms = [tap * weights_ref[w, h // 2, rows, :] for w, tap in enumerate(taps)]
            while len(terms) > 1:
                terms = [a + b for a, b in zip(terms[::2], terms[1::2])]
            sums[h // 2, rows, :] = terms[0]
            return carry

        lax.fori_loop(0, 8, body, 0)
    for odd in range(2):
        gram_ref[pl.ds(odd, LANES, stride=2), :] = sums[odd].T


def call(kernel, out_shape, specs, scratch=(), flops=0):
    spaces = {"s": pltpu.SMEM, "v": pltpu.VMEM, "h": pltpu.HBM}
    vmem = pl.BlockSpec(memory_space=pltpu.VMEM)
    return pl.pallas_call(
        kernel,
        out_shape=out_shape,
        in_specs=[pl.BlockSpec(memory_space=spaces[spec]) for spec in specs],
        out_specs=jax.tree.map(lambda shape: vmem, out_shape),
        scratch_shapes=list(scratch),
        compiler_params=pltpu.CompilerParams(vmem_limit_bytes=40 * MIB),
        cost_estimate=pl.CostEstimate(flops=flops, bytes_accessed=4 * MIB, transcendentals=0),
    )


def struct(shape, kind=F32):
    return jax.ShapeDtypeStruct(tuple(shape), kind)


def segment_transform(devices, place, samples):
    points = samples.size // 2
    table, twiddle = segment_tables(), twiddle_table()
    return call(
        functools.partial(segment_kernel, devices),
        struct((points * 2 // LANES, LANES)),
        "shhh",
        [
            pltpu.VMEM(samples.shape, F32),
            pltpu.VMEM(table.shape, BF16),
            pltpu.VMEM(twiddle.shape, F32),
            pltpu.VMEM((2, 4, 2 * LANES, SIDE), BF16),
            pltpu.VMEM((2, 4, SIDE, 2 * LANES), BF16),
            pltpu.SemaphoreType.DMA((13,)),
        ],
        3 * 2 * 8 * SIDE * SIDE * LANES,
    )(place, samples, jnp.asarray(table), jnp.asarray(twiddle))


def device_transform(devices, received):
    return call(
        functools.partial(device_kernel, devices),
        struct((received.shape[0] // 2, LANES)),
        "vv",
        flops=3 * 2 * 2 * devices * received.shape[0] // 2 * LANES,
    )(received, jnp.asarray(device_table(devices)))


def gram_tables(devices, place, index, offset):
    square = (LANES, LANES)
    return call(
        functools.partial(gram_tables_kernel, devices),
        (struct((4, 4) + square), struct((2,) + square, jnp.int32), struct((2 * HALF, 2) + square)),
        "svv",
        flops=1 << 26,
    )(place, index, offset)


def ends(timed, gains):
    tile = struct((HALF, LANES))
    return call(ends_kernel, (tile, tile), "vv")(timed, gains)


def times_block(timed, gains):
    return call(
        times_kernel, (struct(timed.shape), struct((4, SIDE, LANES))), "vv", flops=1 << 22
    )(timed, gains)


def gram_sums(before, after, held, ids, weights):
    return call(
        gram_kernel,
        struct((2 * LANES, LANES)),
        "vvvvv",
        [pltpu.VMEM((4, SIDE + 2 * HALF, LANES), F32), pltpu.VMEM((2, LANES, LANES), F32)],
        1 << 24,
    )(before, after, held, ids, weights)


def local(samples, gram_index, gram_offset):
    inner, outer = lax.axis_size("inner"), lax.axis_size("outer")
    devices = inner * outer
    place = (lax.axis_index("inner") * outer + lax.axis_index("outer")).astype(jnp.int32)
    spot = place.reshape(1)
    points = samples.shape[2]
    parts = segment_transform(devices, spot, samples.reshape(2, points // LANES, LANES))
    received = lax.all_to_all(parts.reshape(devices, 16, LANES), AXES, 0, 0, tiled=True)
    real = device_transform(devices, received.reshape(16 * devices, LANES))
    rows = gram_index.shape[0] // LANES
    real, index, offset = lax.optimization_barrier(
        (real, gram_index.reshape(rows, LANES), gram_offset.reshape(rows, LANES))
    )
    timed = lax.all_to_all(real.reshape(devices, 8, LANES), AXES, 0, 0, tiled=True)
    gains, ids, weights = gram_tables(devices, spot, index, offset)
    timed = timed.reshape(8 * devices, LANES)
    first, last = ends(timed, gains)
    up = [(i, i + 1) for i in range(devices - 1)]
    before = lax.ppermute(last, AXES, up)
    after = lax.ppermute(first, AXES, [(j, i) for i, j in up])
    z_field, held = times_block(timed, gains)
    gram = gram_sums(before, after, held, ids, weights)
    return z_field.reshape(points), gram.reshape(-1)


def solution(mesh):
    return jax.shard_map(
        local,
        mesh=mesh,
        in_specs=(P(None, AXES, None), P(AXES), P(AXES)),
        out_specs=(P(AXES), P(AXES)),
        check_vma=False,
    )
```

time: 138 us -> 135 us (0.978)
  waiting for transfers between devices: 30.9 us -> 27.3 us
  other arithmetic: 3.53 us -> 0 us
  local copies, waits for them, and re-layouts: 3.55 us -> 6.36 us
  Pallas kernels: 11.9 us -> 13.3 us
    all_to_all x1, waiting for transfers between devices: 30.9 us -> 27.3 us  [local(): lax.all_to_all(real.reshape(devices, 8, LANES), AXES, 0, 0, tiled=True)]
    unnamed x10 -> x16, local copies, waits for them, and re-layouts: 2.82 us -> 6.36 us
    scatter-add x2 -> x0, other arithmetic: 2.88 us -> none  [local(): gram.at[:head.shape[0]].add(head).at[gram.shape[0] - tail.shape[0]:]]
    pallas_call x3 -> x6, Pallas kernels: 11.9 us -> 13.3 us  [the longest x1 4.89 us: segment_transform(): call(functools.partial(segment_kernel, devices), struct((points * 2 // LA...]
  transfers between devices with their start and end apart: 3 -> 3, of which waited for: 1 -> 1; matrix products, arithmetic and copies ran while one was open for 1% -> 0% of each run, Pallas kernels for 3% -> 2%
where the time goes in v1:
time: 135 us
  blocking collectives  67.8 us (50%)
  waiting for transfers between devices  27.3 us (20%)
  starting transfers between devices  19.1 us (14%)
  Pallas kernels  13.3 us (10%)
  local copies, waits for them, and re-layouts  6.36 us (5%)
    all_to_all x1, blocking collectives, local(): lax.all_to_all(parts.reshape(devices, 16, LANES), AXES, 0, 0, tiled=True)  67.8 us
    all_to_all x1, waiting for transfers between devices, local(): lax.all_to_all(real.reshape(devices, 8, LANES), AXES, 0, 0, tiled=True)  27.3 us
    ppermute x1, starting transfers between devices, local(): after = lax.ppermute(first, AXES, [(j, i) for i, j in up])  7.77 us
    all_to_all x1, starting transfers between devices, local(): lax.all_to_all(real.reshape(devices, 8, LANES), AXES, 0, 0, tiled=True)  7.26 us
    unnamed x16, local copies, waits for them, and re-layouts  6.36 us
    pallas_call x1, Pallas kernels, segment_transform(): call(functools.partial(segment_kernel, devices), struct((points * 2 // LA...  4.89 us
    ppermute x1, starting transfers between devices, local(): before = lax.ppermute(last, AXES, up)  4.08 us
  transfers between devices with their start and end apart: 3, of which 1 were waited for; matrix products, arithmetic and copies ran while one was open for 0% of the time, Pallas kernels for 2%

profile of v1, /device:TPU:1, one launch (start us, length us, event | category | flops | bytes accessed | tf_op | source)
XLA Modules:
  0.0 134.6 jit_solution(515280143005229321)
XLA Ops:
  0.6 0.0 copy-start.2
  0.6 1.6 %copy-done.2 = f32[2,1,262144]{2,1,0:T(1,128)S(1)} copy-done((f32[2,1,262144]{2,1,0:T(1,128)S(1)}, f32[2,1,262144]{2,1,0:T(1,128)}, u32[]{:S(2)}) %copy-start.2) | copy-done | bytes 2097176
  2.2 0.0 copy-start.3
  2.2 1.6 %copy-done.3 = f32[2,512,512]{2,1,0:T(8,128)S(1)} copy-done((f32[2,512,512]{2,1,0:T(8,128)S(1)}, f32[2,512,512]{2,1,0:T(8,128)}, u32[]{:S(2)}) %copy-start.3) | copy-done | bytes 2097176
  3.8 0.0 copy-start.4
  3.8 1.2 copy-done.4
  5.0 4.9 %shard_map.77 = f32[4096,128]{1,0:T(8,128)S(1)} custom-call(s32[1]{0:T(128)} %bitcast.place_ref, f32[2,2048,128]{2,1,0:T(8,128)S(1)} %bitcast.14, bf16[2,4,256,256]{3,2,1,0:T(8,128)(2,1)S(1)} %copy-done.4, f32[2,512,512]{2,1,0:T(8,128)S(1)} %copy-done.3), custom_call_target="tpu_custom_call" | custom-call | flops 1610612736 | bytes 4194304 | tf_op jit(solution)/shard_map/pallas_call | solution.py:287
  9.9 0.0 copy-start.5
  10.0 67.8 %all_to_all.10 = f32[256,16,128]{2,1,0:T(8,128)S(1)} all-to-all(f32[256,16,128]{2,1,0:T(8,128)S(1)} %bitcast.13), channel_id=1, replica_groups=mesh['inner'=32,'outer'=8] {'inner','outer'}, dimensions={0} | all-to-all | bytes 4194304 | tf_op jit(solution)/shard_map/all_to_all | solution.py:350
  77.8 0.0 copy-done.5
  77.8 0.0 copy-start.6
  77.8 0.0 copy-start.7
  77.8 2.5 %shard_map.78 = f32[2048,128]{1,0:T(8,128)} custom-call(f32[4096,128]{1,0:T(8,128)S(1)} %bitcast.12, bf16[2,256,512]{2,1,0:T(8,128)(2,1)S(1)} %copy-done.5), custom_call_target="tpu_custom_call" | custom-call | flops 805306368 | bytes 4194304 | tf_op jit(solution)/shard_map/pallas_call | solution.py:304
  80.2 7.3 %all-to-all-start.1 = ((f32[256,8,128]{2,1,0:T(8,128)}), f32[256,8,128]{2,1,0:T(8,128)S(1)}, u32[]{:S(2)}, u32[]{:S(2)}) async-start(f32[256,8,128]{2,1,0:T(8,128)} %bitcast.6), calls=%async_computation.1 | async-start | bytes 2097152 | tf_op jit(solution)/shard_map/all_to_all | solution.py:356
  87.5 0.0 copy-done.6
  87.5 0.0 copy-done.7
  87.5 1.8 %shard_map.79 = (f32[4,4,128,128]{3,2,1,0:T(8,128)S(1)}, s32[2,128,128]{2,1,0:T(8,128)S(1)}, f32[32,2,128,128]{3,2,1,0:T(8,128)S(1)}) custom-call(s32[1]{0:T(128)} %bitcast.place_ref, s32[256,128]{1,0:T(8,128)S(1)} %bitcast.15, s32[256,128]{1,0:T(8,128)S(1)} %bitcast.16), custom_call_target="tpu_custom_call" | custom-call | flops 67108864 | bytes 4194304 | tf_op jit(solution)/shard_map/pallas_call | solution.py:314
  89.4 0.0 copy-start
  89.4 1.9 %copy-done = f32[32,2,128,128]{3,2,1,0:T(8,128)} copy-done((f32[32,2,128,128]{3,2,1,0:T(8,128)}, f32[32,2,128,128]{3,2,1,0:T(8,128)S(1)}, u32[]{:S(2)}) %copy-start) | copy-done | bytes 4194328
  91.3 27.3 %all-to-all-done.1 = f32[256,8,128]{2,1,0:T(8,128)S(1)} async-done(((f32[256,8,128]{2,1,0:T(8,128)}), f32[256,8,128]{2,1,0:T(8,128)S(1)}, u32[]{:S(2)}, u32[]{:S(2)}) %all-to-all-start.1) | async-done | bytes 1048608 | tf_op jit(solution)/shard_map/all_to_all | solution.py:356
  118.6 0.0 copy-start.1
  118.7 4.1 %collective-permute-start = (f32[16,128]{1,0:T(8,128)S(1)}, f32[16,128]{1,0:T(8,128)S(1)}, u32[]{:S(2)}, u32[]{:S(2)}) collective-permute-start(f32[16,128]{1,0:T(8,128)S(1)} %get-tuple-element.17), channel_id=1, source_target_pairs={{0,1},{1,2},{2,3},{3,4},{4,5},{5,6},{6,7},{7,8},{8,9},{9,10},{10,1... | collective-permute-start | bytes 24584 | tf_op jit(solution)/shard_map/ppermute | solution.py:361
  122.7 7.8 %collective-permute-start.1 = (f32[16,128]{1,0:T(8,128)S(1)}, f32[16,128]{1,0:T(8,128)S(1)}, u32[]{:S(2)}, u32[]{:S(2)}) collective-permute-start(f32[16,128]{1,0:T(8,128)S(1)} %get-tuple-element.18), channel_id=1, source_target_pairs={{1,0},{2,1},{3,2},{4,3},{5,4},{6,5},{7,6},{8,7},{9,8},{10,9},{11,1... | collective-permute-start | bytes 24584 | tf_op jit(solution)/shard_map/ppermute | solution.py:362
  130.5 1.5 %shard_map.80 = (f32[2048,128]{1,0:T(8,128)}, f32[4,512,128]{2,1,0:T(8,128)S(1)}) custom-call(f32[2048,128]{1,0:T(8,128)S(1)} %bitcast.11, f32[4,4,128,128]{3,2,1,0:T(8,128)S(1)} %get-tuple-element.15.gain_ref), custom_call_target="tpu_custom_call" | custom-call | flops 4194304 | bytes 4194304 | tf_op jit(solution)/shard_map/pallas_call | solution.py:328
  132.0 0.0 collective-permute-done.before_ref
  132.0 0.0 collective-permute-done.1.after_ref
  132.0 0.0 copy-done.1
  132.0 2.6 %shard_map.82 = f32[256,128]{1,0:T(8,128)} custom-call(f32[16,128]{1,0:T(8,128)S(1)} %collective-permute-done.before_ref, f32[16,128]{1,0:T(8,128)S(1)} %collective-permute-done.1.after_ref, f32[4,512,128]{2,1,0:T(8,128)S(1)} %get-tuple-element.19.held_ref, s32[2,128,128]{2,1,0:T(8,128)S(1)} %get-tuple-element.20.ids_ref, f32[32,2,128,128]{3,2,1,0:T(8,128)S(1)} %copy-done.1), custom_call_target="tpu_custom_call" | custom-call | flops 16777216 | bytes 4194304 | tf_op jit(solution)/shard_map/pallas_call | solution.py:334
  (1 shorter events, 0.0 us)
Async XLA Ops:
  0.6 1.6 %copy-start.2 = (f32[2,1,262144]{2,1,0:T(1,128)S(1)}, f32[2,1,262144]{2,1,0:T(1,128)}, u32[]{:S(2)}) copy-start(f32[2,1,262144]{2,1,0:T(1,128)} %param.6) | copy-start | bytes 6291460
  2.2 1.6 %copy-start.3 = (f32[2,512,512]{2,1,0:T(8,128)S(1)}, f32[2,512,512]{2,1,0:T(8,128)}, u32[]{:S(2)}) copy-start(f32[2,512,512]{2,1,0:T(8,128)} %constant.18.clone.twiddle_hbm) | copy-start | bytes 6291460
  3.8 1.2 copy-start.4
  9.9 67.8 %copy-start.5 = (bf16[2,256,512]{2,1,0:T(8,128)(2,1)S(1)}, bf16[2,256,512]{2,1,0:T(8,128)(2,1)}, u32[]{:S(2)}) copy-start(bf16[2,256,512]{2,1,0:T(8,128)(2,1)} %constant.19.clone.table_ref) | copy-start | bytes 1572868
  77.8 9.7 %copy-start.6 = (s32[32768]{0:T(1024)S(1)}, s32[32768]{0:T(1024)}, u32[]{:S(2)}) copy-start(s32[32768]{0:T(1024)} %param.7) | copy-start | bytes 393220
  77.8 9.8 %copy-start.7 = (s32[32768]{0:T(1024)S(1)}, s32[32768]{0:T(1024)}, u32[]{:S(2)}) copy-start(s32[32768]{0:T(1024)} %param.8) | copy-start | bytes 393220
  80.2 38.4 %all-to-all-start.1 = ((f32[256,8,128]{2,1,0:T(8,128)}), f32[256,8,128]{2,1,0:T(8,128)S(1)}, u32[]{:S(2)}, u32[]{:S(2)}) async-start(f32[256,8,128]{2,1,0:T(8,128)} %bitcast.6), calls=%async_computation.1 | async-start | bytes 2097152 | tf_op jit(solution)/shard_map/all_to_all | solution.py:356
  89.4 1.9 %copy-start = (f32[32,2,128,128]{3,2,1,0:T(8,128)}, f32[32,2,128,128]{3,2,1,0:T(8,128)S(1)}, u32[]{:S(2)}) copy-start(f32[32,2,128,128]{3,2,1,0:T(8,128)S(1)} %get-tuple-element.21.weights_ref) | copy-start | bytes 12582916
  118.6 13.4 %copy-start.1 = (f32[32,2,128,128]{3,2,1,0:T(8,128)S(1)}, f32[32,2,128,128]{3,2,1,0:T(8,128)}, u32[]{:S(2)}) copy-start(f32[32,2,128,128]{3,2,1,0:T(8,128)} %copy-done) | copy-start | bytes 12582916
  118.7 13.4 %collective-permute-start = (f32[16,128]{1,0:T(8,128)S(1)}, f32[16,128]{1,0:T(8,128)S(1)}, u32[]{:S(2)}, u32[]{:S(2)}) collective-permute-start(f32[16,128]{1,0:T(8,128)S(1)} %get-tuple-element.17), channel_id=1, source_target_pairs={{0,1},{1,2},{2,3},{3,4},{4,5},{5,6},{6,7},{7,8},{8,9},{9,10},{10,1... | collective-permute-start | bytes 24584 | tf_op jit(solution)/shard_map/ppermute | solution.py:361
  122.7 9.3 %collective-permute-start.1 = (f32[16,128]{1,0:T(8,128)S(1)}, f32[16,128]{1,0:T(8,128)S(1)}, u32[]{:S(2)}, u32[]{:S(2)}) collective-permute-start(f32[16,128]{1,0:T(8,128)S(1)} %get-tuple-element.18), channel_id=1, source_target_pairs={{1,0},{2,1},{3,2},{4,3},{5,4},{6,5},{7,6},{8,7},{9,8},{10,9},{11,1... | collective-permute-start | bytes 24584 | tf_op jit(solution)/shard_map/ppermute | solution.py:362

commit v2 on v1

--- a/solution.py
+++ b/solution.py
@@ -16,6 +16,7 @@
 SPREAD = HALF / 2.0
 SIDE = 512
 LANES = 128
+ROWS = 9
 AXES = ("inner", "outer")
 F32 = jnp.float32
 BF16 = jnp.bfloat16
@@ -77,8 +78,8 @@
 
 
 def segment_kernel(
-    devices, place_ref, x_hbm, table_hbm, twiddle_hbm, out_ref,
-    x_ref, table_ref, twiddle_ref, first_ref, second_ref, sems,
+    devices, place_ref, x_hbm, table_hbm, twiddle_hbm, out_hbm,
+    x_ref, table_ref, twiddle_ref, first_ref, second_ref, out_ref, sems,
 ):
     place = place_ref[0]
     length = SIDE * SIDE * devices
@@ -110,44 +111,56 @@
                 first_ref[0, g, rows, cols] = high
                 first_ref[1, g, rows, cols] = low
     copies[8].wait()
-    for g in range(4):
-        done = dot3((table_ref[0, g], table_ref[1, g]), (first_ref[0, g], first_ref[1, g]))
-        u = 4 * lax.broadcasted_iota(jnp.int32, (LANES, LANES), 0) + g
-        angle = (place * u).astype(F32) * (-2.0 * math.pi / length)
-        square = angle * angle
-        turn = (
-            1.0 - square * (0.5 - square * (1.0 / 24.0)),
-            angle * (1.0 - square * (1.0 / 6.0 - square * (1.0 / 120.0))),
-        )
-        rows = pl.ds(LANES * g, LANES)
-        grid = []
-        copies[9 + g].wait()
-        for j in range(4):
-            cols = slice(LANES * j, LANES * (j + 1))
-            both = times((twiddle_ref[0, rows, cols], twiddle_ref[1, rows, cols]), turn)
-            grid.append(times((done[:LANES, cols], done[LANES:, cols]), both))
-        for h, pair in enumerate(quarter(grid)):
+    for half in range(2):
+        for upper in range(2):
+            g = 2 * upper + half
+            done = dot3((table_ref[0, g], table_ref[1, g]), (first_ref[0, g], first_ref[1, g]))
+            u = 4 * lax.broadcasted_iota(jnp.int32, (LANES, LANES), 0) + g
+            angle = (place * u).astype(F32) * (-2.0 * math.pi / length)
+            square = angle * angle
+            turn = (
+                1.0 - square * (0.5 - square * (1.0 / 24.0)),
+                angle * (1.0 - square * (1.0 / 6.0 - square * (1.0 / 120.0))),
+            )
+            rows = pl.ds(LANES * g, LANES)
+            grid = []
+            copies[9 + g].wait()
+            for j in range(4):
+                cols = slice(LANES * j, LANES * (j + 1))
+                both = times((twiddle_ref[0, rows, cols], twiddle_ref[1, rows, cols]), turn)
+                grid.append(times((done[:LANES, cols], done[LANES:, cols]), both))
+            for h, pair in enumerate(quarter(grid)):
+                for part in range(2):
+                    high, low = split(pair[part])
+                    rows, cols = pl.ds(LANES * upper, LANES), pl.ds(LANES * part, LANES)
+                    second_ref[0, half, h, rows, cols] = high
+                    second_ref[1, half, h, rows, cols] = low
+        for h in range(4):
+            done = dot3(
+                (second_ref[0, half, h], second_ref[1, half, h]),
+                (table_ref[0, h], table_ref[1, h]),
+                ((1,), (1,)),
+            )
+            v = 4 * lax.broadcasted_iota(jnp.int32, (8, LANES), 1) + h
+            angle = (place * v).astype(F32) * (-2.0 * math.pi * SIDE / length)
+            turn = (jnp.cos(angle)[:1], jnp.sin(angle)[:1])
+            pair = times((done[:, :LANES], done[:, LANES:]), turn)
             for part in range(2):
-                high, low = split(pair[part])
-                cols = pl.ds(LANES * part, LANES)
-                second_ref[0, h, rows, cols] = high
-                second_ref[1, h, rows, cols] = low
-    for h in range(4):
-        done = dot3(
-            (second_ref[0, h], second_ref[1, h]), (table_ref[0, h], table_ref[1, h]), ((1,), (1,))
-        )
-        v = 4 * lax.broadcasted_iota(jnp.int32, (8, LANES), 1) + h
-        angle = (place * v).astype(F32) * (-2.0 * math.pi * SIDE / length)
-        turn = (jnp.cos(angle)[:1], jnp.sin(angle)[:1])
-        pair = times((done[:, :LANES], done[:, LANES:]), turn)
-        for part in range(2):
-            for upper in range(2):
-                out_ref[pl.ds(8 * part + 4 * upper + h, SIDE // 2, stride=16), :] = pair[part][
-                    SIDE // 2 * upper : SIDE // 2 * (upper + 1)
-                ]
+                for upper in range(2):
+                    start = 16 * LANES * half + 8 * part + 4 * upper + h
+                    out_ref[pl.ds(start, LANES, stride=16), :] = pair[part][
+                        LANES * upper : LANES * (upper + 1)
+                    ]
+        rows = pl.ds(16 * LANES * half, 16 * LANES)
+        copy = pltpu.make_async_copy(out_ref.at[rows], out_hbm.at[rows], sems.at[13 + half])
+        copy.start()
+        copies.append(copy)
+    for copy in copies[13:]:
+        copy.wait()
 
 
 def device_kernel(devices, x_ref, table_ref, out_ref):
+    edges = {}
     for block in range(4):
         columns = []
         for e in (2 * block, 2 * block + 1):
@@ -159,7 +172,17 @@
         x = jnp.concatenate(columns, axis=1)
         done = dot3((table_ref[0], table_ref[1]), split(x))
         for i, e in enumerate((2 * block, 2 * block + 1)):
-            out_ref[pl.ds(e, devices, stride=8), :] = done[:, LANES * i : LANES * (i + 1)]
+            values = done[:, LANES * i : LANES * (i + 1)]
+            out_ref[pl.ds(e, devices, stride=ROWS), :] = values
+            if e % 4 in (0, 3):
+                edges[e] = values
+    lane = lax.broadcasted_iota(jnp.int32, (devices, LANES), 1)
+    row = lax.broadcasted_iota(jnp.int32, (devices, LANES), 0)
+    after = jnp.where(lane == 0, edges[0], pltpu.roll(edges[4], 1, 1))
+    before = jnp.where(lane == LANES - 1, edges[3], pltpu.roll(edges[7], LANES - 1, 1))
+    after = jnp.where(row == devices - 1, 0.0, pltpu.roll(after, devices - 1, 0))
+    before = jnp.where(row == 0, 0.0, pltpu.roll(before, 1, 0))
+    out_ref[pl.ds(8, devices, stride=ROWS), :] = jnp.where(lane < 2, after, before)
 
 
 def gain(devices, place, position):
@@ -168,7 +191,9 @@
     return length ** (-0.5) * jnp.exp(RATE * centred * centred)
 
 
-def gram_tables_kernel(devices, place_ref, index_ref, offset_ref, gain_ref, ids_ref, weights_ref):
+def gram_tables_kernel(
+    devices, place_ref, index_ref, offset_ref, gain_ref, edge_ref, ids_ref, weights_ref
+):
     place = place_ref[0]
     t = lax.broadcasted_iota(jnp.int32, (LANES, LANES), 0)
     lane = lax.broadcasted_iota(jnp.int32, (LANES, LANES), 1)
@@ -176,6 +201,9 @@
         for g in range(4):
             position = SIDE * (4 * lane + h) + 4 * t + g
             gain_ref[h, g] = gain(devices, place, position)
+    u = t[:HALF]
+    edge_ref[0] = gain(devices, place - 1, u + (SIDE * SIDE - HALF))
+    edge_ref[1] = gain(devices, place + 1, u)
     for odd in range(2):
         ids_ref[odd] = index_ref[pl.ds(odd, LANES, stride=2), :].T
         fraction = offset_ref[pl.ds(odd, LANES, stride=2), :].T.astype(F32) * (1.0 / UPS)
@@ -200,44 +228,36 @@
     weights_ref[HALF - 1, odd] = jnp.where(at_zero, 1.0, sine / jnp.where(at_zero, 1.0, fraction))
 
 
-def ends_kernel(x_ref, gain_ref, first_ref, last_ref):
-    count = HALF // 4
-    for g in range(4):
-        for h, t, out_ref in ((0, 0, first_ref), (3, LANES - count, last_ref)):
-            start = 8 * LANES * (g % 2) + 4 * (g // 2) + h
-            low = t - t % 8
-            raw = x_ref[pl.ds(start + 8 * low, 8, stride=8), :] * gain_ref[h, g, pl.ds(low, 8), :]
-            out_ref[pl.ds(g, count, stride=4), :] = raw[t - low : t - low + count]
-
-
-def times_kernel(x_ref, gain_ref, z_ref, held_ref):
+def times_kernel(x_ref, gain_ref, edge_ref, ids_ref, weights_ref, z_hbm, gram_ref, zs_ref, z_ref, ends_ref, sums, sem):
+    pad = HALF
     for h in range(4):
         for g in range(4):
-            start = 8 * LANES * (g % 2) + 4 * (g // 2) + h
-            raw = x_ref[pl.ds(start, LANES, stride=8), :]
-            held_ref[h, pl.ds(g, LANES, stride=4), :] = raw * gain_ref[h, g]
+            start = ROWS * LANES * (g % 2) + 4 * (g // 2) + h
+            raw = x_ref[pl.ds(start, LANES, stride=ROWS), :]
+            zs_ref[h, pl.ds(pad + g, LANES, stride=4), :] = raw * gain_ref[h, g]
         for block in range(4):
-            z_ref[pl.ds(4 * h + block, LANES, stride=16), :] = held_ref[
-                h, pl.ds(LANES * block, LANES), :
+            z_ref[pl.ds(4 * h + block, LANES, stride=16), :] = zs_ref[
+                h, pl.ds(pad + LANES * block, LANES), :
             ].T
-
-
-def gram_kernel(before_ref, after_ref, held_ref, ids_ref, weights_ref, gram_ref, zs_ref, sums):
-    pad = HALF
-    edge = lax.broadcasted_iota(jnp.int32, (pad, LANES), 1)
+    copy = pltpu.make_async_copy(z_ref, z_hbm, sem)
+    copy.start()
+    for g in range(4):
+        upper = g // 2
+        for side, t, shift in ((0, LANES - 8, 1 + upper), (1, 0, LANES - 1 - upper)):
+            start = ROWS * (LANES * (g % 2) + t) + 8
+            tile = pltpu.roll(x_ref[pl.ds(start, 8, stride=ROWS), :], shift, 1)
+            ends_ref[side, pl.ds(g, 8, stride=4), :] = tile
+    lane = lax.broadcasted_iota(jnp.int32, (pad, LANES), 1)
     for h in range(4):
-        before = held_ref[(h - 1) % 4, pl.ds(SIDE - pad, pad), :]
-        after = held_ref[(h + 1) % 4, pl.ds(0, pad), :]
+        before = zs_ref[(h - 1) % 4, pl.ds(SIDE, pad), :]
+        after = zs_ref[(h + 1) % 4, pl.ds(pad, pad), :]
         if h == 0:
-            before = jnp.where(edge == 0, pltpu.roll(before_ref[...], 1, 1), pltpu.roll(before, 1, 1))
+            edge = ends_ref[0, pl.ds(pad, pad), :] * edge_ref[0]
+            before = jnp.where(lane == 0, edge, pltpu.roll(before, 1, 1))
         if h == 3:
-            after = jnp.where(
-                edge == LANES - 1,
-                pltpu.roll(after_ref[...], LANES - 1, 1),
-                pltpu.roll(after, LANES - 1, 1),
-            )
+            edge = ends_ref[1, pl.ds(0, pad), :] * edge_ref[1]
+            after = jnp.where(lane == LANES - 1, edge, pltpu.roll(after, LANES - 1, 1))
         zs_ref[h, pl.ds(0, pad), :] = before
-        zs_ref[h, pl.ds(pad, SIDE), :] = held_ref[h]
         zs_ref[h, pl.ds(pad + SIDE, pad), :] = after
     for h in range(4):
 
@@ -261,18 +281,21 @@
         lax.fori_loop(0, 8, body, 0)
     for odd in range(2):
         gram_ref[pl.ds(odd, LANES, stride=2), :] = sums[odd].T
-
-
-def call(kernel, out_shape, specs, scratch=(), flops=0):
+    copy.wait()
+
+
+def call(kernel, out_shape, specs, scratch=(), flops=0, limit=16, outs="v"):
     spaces = {"s": pltpu.SMEM, "v": pltpu.VMEM, "h": pltpu.HBM}
-    vmem = pl.BlockSpec(memory_space=pltpu.VMEM)
+    out_specs = [pl.BlockSpec(memory_space=spaces[spec]) for spec in outs]
+    if len(outs) == 1:
+        out_specs = out_specs[0]
     return pl.pallas_call(
         kernel,
         out_shape=out_shape,
         in_specs=[pl.BlockSpec(memory_space=spaces[spec]) for spec in specs],
-        out_specs=jax.tree.map(lambda shape: vmem, out_shape),
+        out_specs=out_specs,
         scratch_shapes=list(scratch),
-        compiler_params=pltpu.CompilerParams(vmem_limit_bytes=40 * MIB),
+        compiler_params=pltpu.CompilerParams(vmem_limit_bytes=limit * MIB),
         cost_estimate=pl.CostEstimate(flops=flops, bytes_accessed=4 * MIB, transcendentals=0),
     )
 
@@ -293,17 +316,20 @@
             pltpu.VMEM(table.shape, BF16),
             pltpu.VMEM(twiddle.shape, F32),
             pltpu.VMEM((2, 4, 2 * LANES, SIDE), BF16),
-            pltpu.VMEM((2, 4, SIDE, 2 * LANES), BF16),
-            pltpu.SemaphoreType.DMA((13,)),
+            pltpu.VMEM((2, 2, 4, 2 * LANES, 2 * LANES), BF16),
+            pltpu.VMEM((points * 2 // LANES, LANES), F32),
+            pltpu.SemaphoreType.DMA((15,)),
         ],
         3 * 2 * 8 * SIDE * SIDE * LANES,
+        60,
+        "h",
     )(place, samples, jnp.asarray(table), jnp.asarray(twiddle))
 
 
 def device_transform(devices, received):
     return call(
         functools.partial(device_kernel, devices),
-        struct((received.shape[0] // 2, LANES)),
+        struct((ROWS * devices, LANES)),
         "vv",
         flops=3 * 2 * 2 * devices * received.shape[0] // 2 * LANES,
     )(received, jnp.asarray(device_table(devices)))
@@ -313,31 +339,34 @@
     square = (LANES, LANES)
     return call(
         functools.partial(gram_tables_kernel, devices),
-        (struct((4, 4) + square), struct((2,) + square, jnp.int32), struct((2 * HALF, 2) + square)),
+        (
+            struct((4, 4) + square),
+            struct((2, HALF, LANES)),
+            struct((2,) + square, jnp.int32),
+            struct((2 * HALF, 2) + square),
+        ),
         "svv",
         flops=1 << 26,
+        outs="vvvv",
     )(place, index, offset)
 
 
-def ends(timed, gains):
-    tile = struct((HALF, LANES))
-    return call(ends_kernel, (tile, tile), "vv")(timed, gains)
-
-
-def times_block(timed, gains):
+def times_block(timed, tables):
+    rows = SIDE * SIDE // LANES
     return call(
-        times_kernel, (struct(timed.shape), struct((4, SIDE, LANES))), "vv", flops=1 << 22
-    )(timed, gains)
-
-
-def gram_sums(before, after, held, ids, weights):
-    return call(
-        gram_kernel,
-        struct((2 * LANES, LANES)),
+        times_kernel,
+        (struct((rows, LANES)), struct((2 * LANES, LANES))),
         "vvvvv",
-        [pltpu.VMEM((4, SIDE + 2 * HALF, LANES), F32), pltpu.VMEM((2, LANES, LANES), F32)],
+        [
+            pltpu.VMEM((4, SIDE + 2 * HALF, LANES), F32),
+            pltpu.VMEM((rows, LANES), F32),
+            pltpu.VMEM((2, 2 * HALF, LANES), F32),
+            pltpu.VMEM((2, LANES, LANES), F32),
+            pltpu.SemaphoreType.DMA(()),
+        ],
         1 << 24,
-    )(before, after, held, ids, weights)
+        outs="hv",
+    )(timed, *tables)
 
 
 def local(samples, gram_index, gram_offset):
@@ -353,15 +382,9 @@
     real, index, offset = lax.optimization_barrier(
         (real, gram_index.reshape(rows, LANES), gram_offset.reshape(rows, LANES))
     )
-    timed = lax.all_to_all(real.reshape(devices, 8, LANES), AXES, 0, 0, tiled=True)
-    gains, ids, weights = gram_tables(devices, spot, index, offset)
-    timed = timed.reshape(8 * devices, LANES)
-    first, last = ends(timed, gains)
-    up = [(i, i + 1) for i in range(devices - 1)]
-    before = lax.ppermute(last, AXES, up)
-    after = lax.ppermute(first, AXES, [(j, i) for i, j in up])
-    z_field, held = times_block(timed, gains)
-    gram = gram_sums(before, after, held, ids, weights)
+    timed = lax.all_to_all(real.reshape(-1), AXES, 0, 0, tiled=True)
+    tables = gram_tables(devices, spot, index, offset)
+    z_field, gram = times_block(timed.reshape(ROWS * devices, LANES), tables)
     return z_field.reshape(points), gram.reshape(-1)
 
 

time: 135 us -> 125 us (0.926)
  starting transfers between devices: 19.1 us -> 7.25 us
  waiting for transfers between devices: 27.3 us -> 29.9 us
  local copies, waits for them, and re-layouts: 6.36 us -> 4.13 us
    ppermute x2 -> x0, starting transfers between devices: 11.8 us -> none  [the longest x1 7.77 us: local(): after = lax.ppermute(first, AXES, [(j, i) for i, j in up])]
    all_to_all x1, waiting for transfers between devices: 27.3 us -> 29.9 us  [local(): timed = lax.all_to_all(real.reshape(-1), AXES, 0, 0, tiled=True)]
    unnamed x16 -> x10, local copies, waits for them, and re-layouts: 6.36 us -> 4.13 us
    pallas_call x1, Pallas kernels: 4.89 us -> 7.04 us  [segment_transform(): call(functools.partial(segment_kernel, devices), struct((points * 2 // LA...]
    pallas_call x4 -> x2, Pallas kernels: 6.6 us -> 5.56 us  [the longest x1 3.02 us: times_block(): call(times_kernel, (struct((rows, LANES)), struct((2 * LANES, LANES))), '...]
  transfers between devices with their start and end apart: 3 -> 1, of which waited for: 1 -> 1; matrix products, arithmetic and copies ran while one was open for 0% -> 0% of each run, Pallas kernels for 2% -> 1%
where the time goes in v2:
time: 125 us; the launch traced here: 124 us
  blocking collectives  68 us (54%)
  waiting for transfers between devices  29.9 us (24%)
  Pallas kernels  14.4 us (12%)
  starting transfers between devices  7.25 us (6%)
  local copies, waits for them, and re-layouts  4.13 us (3%)
    all_to_all x1, blocking collectives, local(): lax.all_to_all(parts.reshape(devices, 16, LANES), AXES, 0, 0, tiled=True)  68 us
    all_to_all x1, waiting for transfers between devices, local(): timed = lax.all_to_all(real.reshape(-1), AXES, 0, 0, tiled=True)  29.9 us
    all_to_all x1, starting transfers between devices, local(): timed = lax.all_to_all(real.reshape(-1), AXES, 0, 0, tiled=True)  7.25 us
    pallas_call x1, Pallas kernels, segment_transform(): call(functools.partial(segment_kernel, devices), struct((points * 2 // LA...  7.04 us
    unnamed x10, local copies, waits for them, and re-layouts  4.13 us
    pallas_call x1, Pallas kernels, times_block(): call(times_kernel, (struct((rows, LANES)), struct((2 * LANES, LANES))), '...  3.02 us
    pallas_call x1, Pallas kernels, device_transform(): call(functools.partial(device_kernel, devices), struct((ROWS * devices, L...  2.54 us
  transfers between devices with their start and end apart: 1, of which 1 were waited for; matrix products, arithmetic and copies ran while one was open for 0% of the time, Pallas kernels for 1%

profile of v2, /device:TPU:1, one launch (start us, length us, event | category | flops | bytes accessed | tf_op | source)
XLA Modules:
  0.0 124.5 jit_solution(2909486863152124798)
XLA Ops:
  0.6 7.0 %shard_map.77 = f32[4096,128]{1,0:T(8,128)} custom-call(s32[1]{0:T(128)} %bitcast.place_ref, f32[2,2048,128]{2,1,0:T(8,128)} %bitcast.15, bf16[2,4,256,256]{3,2,1,0:T(8,128)(2,1)} %constant.17.clone.table_hbm, f32[2,512,512]{2,1,0:T(8,128)} %constant.18.clone.twiddle_hbm), custom_call_target="tpu_custom_call" | custom-call | flops 1610612736 | bytes 4194304 | tf_op jit(solution)/shard_map/pallas_call | solution.py:310
  7.7 0.0 copy-start.2
  7.7 68.0 %all_to_all.14 = f32[256,16,128]{2,1,0:T(8,128)S(1)} all-to-all(f32[256,16,128]{2,1,0:T(8,128)} %bitcast.14), channel_id=1, replica_groups=mesh['inner'=32,'outer'=8] {'inner','outer'}, dimensions={0} | all-to-all | bytes 4194304 | tf_op jit(solution)/shard_map/all_to_all | solution.py:379
  75.7 0.0 copy-done.2
  75.7 2.5 %shard_map.78 = f32[2304,128]{1,0:T(8,128)} custom-call(f32[4096,128]{1,0:T(8,128)S(1)} %bitcast.10, bf16[2,256,512]{2,1,0:T(8,128)(2,1)S(1)} %copy-done.2), custom_call_target="tpu_custom_call" | custom-call | flops 805306368 | bytes 4194304 | tf_op jit(solution)/shard_map/pallas_call | solution.py:330
  78.3 0.0 copy-start.3
  78.3 0.0 copy-start.4
  78.3 7.3 %all-to-all-start.1 = ((f32[256,1152,1]{1,2,0:T(1,128)}), f32[256,1152,1]{1,2,0:T(1,128)S(1)}, u32[]{:S(2)}, u32[]{:S(2)}) async-start(f32[256,1152,1]{1,2,0:T(1,128)} %bitcast.6), calls=%async_computation.1 | async-start | bytes 2359296 | tf_op jit(solution)/shard_map/all_to_all | solution.py:385
  85.5 0.0 copy-done.3
  85.5 0.0 copy-done.4
  85.5 1.8 %shard_map.79 = (f32[4,4,128,128]{3,2,1,0:T(8,128)S(1)}, f32[2,16,128]{2,1,0:T(8,128)S(1)}, s32[2,128,128]{2,1,0:T(8,128)S(1)}, f32[32,2,128,128]{3,2,1,0:T(8,128)S(1)}) custom-call(s32[1]{0:T(128)} %bitcast.place_ref, s32[256,128]{1,0:T(8,128)S(1)} %bitcast.12, s32[256,128]{1,0:T(8,128)S(1)} %bitcast.13), custom_call_target="tpu_custom_call" | custom-call | flops 67108864 | bytes 4194304 | tf_op jit(solution)/shard_map/pallas_call | solution.py:340
  87.4 0.0 copy-start
  87.4 1.9 %copy-done = f32[32,2,128,128]{3,2,1,0:T(8,128)} copy-done((f32[32,2,128,128]{3,2,1,0:T(8,128)}, f32[32,2,128,128]{3,2,1,0:T(8,128)S(1)}, u32[]{:S(2)}) %copy-start) | copy-done | bytes 4194328
  89.3 29.9 %all-to-all-done.1 = f32[256,1152,1]{1,2,0:T(1,128)S(1)} async-done(((f32[256,1152,1]{1,2,0:T(1,128)}), f32[256,1152,1]{1,2,0:T(1,128)S(1)}, u32[]{:S(2)}, u32[]{:S(2)}) %all-to-all-start.1) | async-done | bytes 1179680 | tf_op jit(solution)/shard_map/all_to_all | solution.py:385
  119.3 0.0 copy-start.1
  119.3 2.2 %copy-done.1 = f32[32,2,128,128]{3,2,1,0:T(8,128)S(1)} copy-done((f32[32,2,128,128]{3,2,1,0:T(8,128)S(1)}, f32[32,2,128,128]{3,2,1,0:T(8,128)}, u32[]{:S(2)}) %copy-start.1) | copy-done | bytes 4194328
  121.4 3.0 %shard_map.80 = (f32[2048,128]{1,0:T(8,128)}, f32[256,128]{1,0:T(8,128)}) custom-call(f32[2304,128]{1,0:T(8,128)S(1)} %bitcast.11, f32[4,4,128,128]{3,2,1,0:T(8,128)S(1)} %get-tuple-element.14.gain_ref, f32[2,16,128]{2,1,0:T(8,128)S(1)} %get-tuple-element.15.edge_ref, s32[2,128,128]{2,1,0:T(8,128)S(1)} %get-tuple-element.16.ids_ref, ...), custom_call_target="tpu_custom_call" | custom-call | flops 16777216 | bytes 4194304 | tf_op jit(solution)/shard_map/pallas_call | solution.py:356
Async XLA Ops:
  7.7 68.0 %copy-start.2 = (bf16[2,256,512]{2,1,0:T(8,128)(2,1)S(1)}, bf16[2,256,512]{2,1,0:T(8,128)(2,1)}, u32[]{:S(2)}) copy-start(bf16[2,256,512]{2,1,0:T(8,128)(2,1)} %constant.19.clone.table_ref) | copy-start | bytes 1572868
  78.3 7.3 %copy-start.3 = (s32[32768]{0:T(1024)S(1)}, s32[32768]{0:T(1024)}, u32[]{:S(2)}) copy-start(s32[32768]{0:T(1024)} %param.7) | copy-start | bytes 393220
  78.3 7.3 %copy-start.4 = (s32[32768]{0:T(1024)S(1)}, s32[32768]{0:T(1024)}, u32[]{:S(2)}) copy-start(s32[32768]{0:T(1024)} %param.8) | copy-start | bytes 393220
  78.3 41.0 %all-to-all-start.1 = ((f32[256,1152,1]{1,2,0:T(1,128)}), f32[256,1152,1]{1,2,0:T(1,128)S(1)}, u32[]{:S(2)}, u32[]{:S(2)}) async-start(f32[256,1152,1]{1,2,0:T(1,128)} %bitcast.6), calls=%async_computation.1 | async-start | bytes 2359296 | tf_op jit(solution)/shard_map/all_to_all | solution.py:385
  87.4 1.9 %copy-start = (f32[32,2,128,128]{3,2,1,0:T(8,128)}, f32[32,2,128,128]{3,2,1,0:T(8,128)S(1)}, u32[]{:S(2)}) copy-start(f32[32,2,128,128]{3,2,1,0:T(8,128)S(1)} %get-tuple-element.17.weights_ref) | copy-start | bytes 12582916
  119.3 2.2 %copy-start.1 = (f32[32,2,128,128]{3,2,1,0:T(8,128)S(1)}, f32[32,2,128,128]{3,2,1,0:T(8,128)}, u32[]{:S(2)}) copy-start(f32[32,2,128,128]{3,2,1,0:T(8,128)} %copy-done) | copy-start | bytes 12582916

commit v3 on v2

v3 whole, which is shorter than its diff:
```python
import functools
import math

import jax
import jax.numpy as jnp
import numpy as np
from jax import lax
from jax.experimental import pallas as pl
from jax.experimental.pallas import tpu as pltpu
from jax.sharding import PartitionSpec as P

GAP = 8
HALF = 16
UPS = 32
RATE = 4.0
SPREAD = HALF / 2.0
SIDE = 512
LANES = 128
KEPT = 13
ROWS = 9
AXES = ("inner", "outer")
F32 = jnp.float32
BF16 = jnp.bfloat16
MIB = 1 << 20


def halves(table):
    high = table.astype(jnp.bfloat16)
    low = (table - high.astype(np.float64)).astype(jnp.bfloat16)
    return np.stack([high, low])


def device_table(devices):
    n = np.arange(devices)
    angle = 2.0 * np.pi * (n[:, None] * n[None, :] % devices) / devices
    return halves(np.concatenate([np.cos(angle), np.sin(angle)], axis=1))


def split(x):
    high = x.astype(BF16)
    return high, (x - high.astype(F32)).astype(BF16)


def dot(a, b, dims):
    return lax.dot_general(a, b, (dims, ((), ())), preferred_element_type=F32)


def dot3(a, b, dims=((1,), (0,))):
    (a_high, a_low), (b_high, b_low) = a, b
    return dot(a_high, b_high, dims) + (dot(a_high, b_low, dims) + dot(a_low, b_high, dims))


def quarter(parts):
    (r0, i0), (r1, i1), (r2, i2), (r3, i3) = parts
    ar, ai, br, bi = r0 + r2, i0 + i2, r0 - r2, i0 - i2
    cr, ci, er, ei = r1 + r3, i1 + i3, r1 - r3, i1 - i3
    return [(ar + cr, ai + ci), (br + ei, bi - er), (ar - cr, ai - ci), (br - ei, bi + er)]


def times(a, b):
    return a[0] * b[0] - a[1] * b[1], a[0] * b[1] + a[1] * b[0]


def unit(count, period):
    half = period // 2
    near = ((count + half) & (period - 1)) - half
    angle = near.astype(F32) * (0.5 * math.pi / period)
    square = angle * angle
    sine, cosine = 1.0, 1.0
    for n in (4, 3, 2, 1):
        sine = 1.0 - square * (1.0 / ((2 * n) * (2 * n + 1))) * sine
    for n in (5, 4, 3, 2, 1):
        cosine = 1.0 - square * (1.0 / ((2 * n - 1) * (2 * n))) * cosine
    sine = angle * sine
    for _ in range(2):
        sine, cosine = 2.0 * sine * cosine, 1.0 - 2.0 * sine * sine
    return cosine, -sine


def segment_kernel(devices, place_ref, x_ref, out_ref, table_ref, first_ref, second_ref):
    place = place_ref[0]
    points = SIDE * SIDE
    row = lax.broadcasted_iota(jnp.int32, (LANES, LANES), 0)
    lane = lax.broadcasted_iota(jnp.int32, (LANES, LANES), 1)
    line = lax.broadcasted_iota(jnp.int32, (8, LANES), 1)
    whole = unit(row * lane, LANES)
    for g in range(4):
        here = whole
        if g:
            here = times(whole, tuple(x[:1] for x in unit(line * g, SIDE)))
        (cos_high, cos_low), (sin_high, sin_low) = split(here[0]), split(-here[1])
        for k, (cos, sin) in enumerate(((cos_high, sin_high), (cos_low, sin_low))):
            table_ref[k, g, :LANES, :LANES] = cos
            table_ref[k, g, :LANES, LANES:] = sin
            table_ref[k, g, LANES:, :LANES] = -sin
            table_ref[k, g, LANES:, LANES:] = cos
    for j in range(4):
        grid = [
            tuple(x_ref[part, pl.ds(SIDE * i + j, LANES, stride=4), :] for part in range(2))
            for i in range(4)
        ]
        for g, pair in enumerate(quarter(grid)):
            for part in range(2):
                high, low = split(pair[part])
                rows, cols = pl.ds(LANES * part, LANES), pl.ds(LANES * j, LANES)
                first_ref[0, g, rows, cols] = high
                first_ref[1, g, rows, cols] = low
    across = unit(row * lane, points // 4)
    down = unit(row, SIDE)
    for g in range(4):
        done = dot3((table_ref[0, g], table_ref[1, g]), (first_ref[0, g], first_ref[1, g]))
        both = times(across, unit(place * (4 * row + g), points * devices))
        step = down
        if g:
            both = times(both, tuple(x[:1] for x in unit(line * g, points)))
            angle = -2.0 * math.pi * g * LANES / points
            step = times(down, (math.cos(angle), math.sin(angle)))
        grid = []
        for j in range(4):
            cols = slice(LANES * j, LANES * (j + 1))
            if j:
                both = times(both, step)
            grid.append(times((done[:LANES, cols], done[LANES:, cols]), both))
        for h, pair in enumerate(quarter(grid)):
            for part in range(2):
                high, low = split(pair[part])
                rows, cols = pl.ds(LANES * g, LANES), pl.ds(LANES * part, LANES)
                second_ref[0, h, rows, cols] = high
                second_ref[1, h, rows, cols] = low
    for h in range(4):
        done = dot3(
            (second_ref[0, h], second_ref[1, h]), (table_ref[0, h], table_ref[1, h]), ((1,), (1,))
        )
        turn = tuple(x[:1] for x in unit(place * (4 * line + h), SIDE * devices))
        pair = times((done[:, :LANES], done[:, LANES:]), turn)
        for part in range(2):
            for upper in range(2):
                out_ref[pl.ds(8 * part + 4 * upper + h, SIDE // 2, stride=16), :] = pair[part][
                    SIDE // 2 * upper : SIDE // 2 * (upper + 1)
                ]


def device_kernel(devices, x_ref, table_ref, out_ref):
    edges = {}
    for block in range(4):
        columns = []
        for e in (2 * block, 2 * block + 1):
            columns.append(
                jnp.concatenate(
                    [x_ref[pl.ds(8 * part + e, devices, stride=16), :] for part in range(2)], axis=0
                )
            )
        x = jnp.concatenate(columns, axis=1)
        done = dot3((table_ref[0], table_ref[1]), split(x))
        for i, e in enumerate((2 * block, 2 * block + 1)):
            values = done[:, LANES * i : LANES * (i + 1)]
            out_ref[pl.ds(e, devices, stride=ROWS), :] = values
            if e % 4 in (0, 3):
                edges[e] = values
    lane = lax.broadcasted_iota(jnp.int32, (devices, LANES), 1)
    row = lax.broadcasted_iota(jnp.int32, (devices, LANES), 0)
    after = jnp.where(lane == 0, edges[0], pltpu.roll(edges[4], 1, 1))
    before = jnp.where(lane == LANES - 1, edges[3], pltpu.roll(edges[7], LANES - 1, 1))
    after = jnp.where(row == devices - 1, 0.0, pltpu.roll(after, devices - 1, 0))
    before = jnp.where(row == 0, 0.0, pltpu.roll(before, 1, 0))
    out_ref[pl.ds(8, devices, stride=ROWS), :] = jnp.where(lane < 2, after, before)


def gain(devices, place, position):
    length = SIDE * SIDE * devices
    centred = place.astype(F32) / devices + position.astype(F32) / length - 0.5
    return length ** (-0.5) * jnp.exp(RATE * centred * centred)


def gram_tables_kernel(index_ref, offset_ref, code_ref, share_ref, entry_ref):
    for odd in range(2):
        rows = pl.ds(odd, LANES, stride=2)
        code = (offset_ref[rows, :] * GAP + index_ref[rows, :]).T
        code_ref[odd] = code
        fraction = (code >> 3).astype(F32) * (1.0 / UPS)
        for w, share in enumerate(shares_of(fraction)[:KEPT]):
            share_ref[w, odd] = share
    line = lax.broadcasted_iota(jnp.int32, (8, LANES), 1) & (UPS - 1)
    for w, share in enumerate(shares_of(line.astype(F32) * (1.0 / UPS))[KEPT:]):
        entry_ref[w] = share


def shares_of(fraction):
    sine = jnp.sin(math.pi * fraction) * (1.0 / math.pi)
    sine = sine * jnp.exp(fraction * fraction * (-0.5 / (SPREAD * SPREAD)))
    at_zero = fraction == 0.0
    shares = [jnp.where(at_zero, 1.0, sine / jnp.where(at_zero, 1.0, fraction))]
    square = fraction * fraction
    for w in range(1, HALF + 1):
        scale = (-1.0) ** w * math.exp(-0.5 * w * w / (SPREAD * SPREAD))
        shares.append(sine * (scale / (square - w * w)))
    shares.append(jnp.exp(fraction * (1.0 / (SPREAD * SPREAD))))
    shares.append(jnp.exp(fraction * (-1.0 / (SPREAD * SPREAD))))
    return shares


def weighted(taps, shares, fraction):
    up, down = shares[HALF + 1], shares[HALF + 2]
    ups, downs = up, down
    terms = [taps[HALF - 1] * shares[0]]
    for w in range(1, HALF + 1):
        term = (ups * taps[HALF - 1 + w]) * (fraction + w)
        if w < HALF:
            term = term + (downs * taps[HALF - 1 - w]) * (fraction - w)
        terms.append(term * shares[w])
        ups, downs = ups * up, downs * down
    while len(terms) > 1:
        terms = [a + b for a, b in zip(terms[::2], terms[1::2])] + terms[len(terms) & ~1 :]
    return terms[0]


def times_kernel(
    devices, place_ref, x_ref, code_ref, share_ref, entry_ref, z_hbm, gram_ref,
    zs_ref, z_ref, ends_ref, sums, sem,
):
    pad = HALF
    place = place_ref[0]
    length = SIDE * SIDE * devices
    t = lax.broadcasted_iota(jnp.int32, (LANES, LANES), 0)
    line = lax.broadcasted_iota(jnp.int32, (8, LANES), 1)
    for h in range(4):
        begin = SIDE * (4 * line + h)
        base = gain(devices, place, begin)[:1]
        start_c = (place.astype(F32) / devices + begin.astype(F32) / length - 0.5)[:1]
        for g in range(4):
            start = ROWS * LANES * (g % 2) + 4 * (g // 2) + h
            raw = x_ref[pl.ds(start, LANES, stride=ROWS), :]
            du = (4 * t + g).astype(F32) * (1.0 / length)
            x = (du * (2.0 * RATE)) * (start_c + 0.5 * du)
            factor = base + base * (x + 0.5 * x * x)
            zs_ref[h, pl.ds(pad + g, LANES, stride=4), :] = raw * factor
        for block in range(4):
            z_ref[pl.ds(4 * h + block, LANES, stride=16), :] = zs_ref[
                h, pl.ds(pad + LANES * block, LANES), :
            ].T
    copy = pltpu.make_async_copy(z_ref, z_hbm, sem)
    copy.start()
    for g in range(4):
        upper = g // 2
        for side, top, shift in ((0, LANES - 8, 1 + upper), (1, 0, LANES - 1 - upper)):
            start = ROWS * (LANES * (g % 2) + top) + 8
            tile = pltpu.roll(x_ref[pl.ds(start, 8, stride=ROWS), :], shift, 1)
            ends_ref[side, pl.ds(g, 8, stride=4), :] = tile
    lane = lax.broadcasted_iota(jnp.int32, (pad, LANES), 1)
    for h in range(4):
        before = zs_ref[(h - 1) % 4, pl.ds(SIDE, pad), :]
        after = zs_ref[(h + 1) % 4, pl.ds(pad, pad), :]
        if h == 0:
            edge = ends_ref[0, pl.ds(pad, pad), :] * gain(
                devices, place - 1, t[:pad] + (SIDE * SIDE - HALF)
            )
            before = jnp.where(lane == 0, edge, pltpu.roll(before, 1, 1))
        if h == 3:
            edge = ends_ref[1, pl.ds(0, pad), :] * gain(devices, place + 1, t[:pad])
            after = jnp.where(lane == LANES - 1, edge, pltpu.roll(after, LANES - 1, 1))
        zs_ref[h, pl.ds(0, pad), :] = before
        zs_ref[h, pl.ds(pad + SIDE, pad), :] = after
    for h in range(4):

        def body(step, carry, h=h):
            rows = pl.ds(pl.multiple_of(64 * (h % 2) + 8 * step, 8), 8)
            index = code_ref[h // 2, rows, :]
            offset = index >> 3
            fraction = offset.astype(F32) * (1.0 / UPS)
            taps = [
                zs_ref[h, pl.ds(pad + o + 64 * step, 8, stride=8), :]
                for o in range(1 - HALF, HALF + GAP)
            ]
            for bit in (2, 1, 0):
                size = 1 << bit
                chosen = (index >> bit & 1) == 1
                taps = [jnp.where(chosen, b, a) for a, b in zip(taps[:-size], taps[size:])]
            shares = [share_ref[w, h // 2, rows, :] for w in range(KEPT)]
            for w in range(HALF + 3 - KEPT):
                shares.append(jnp.take_along_axis(entry_ref[w], offset, axis=1))
            sums[h // 2, rows, :] = weighted(taps, shares, fraction)
            return carry

        lax.fori_loop(0, 8, body, 0, unroll=4)
    for odd in range(2):
        gram_ref[pl.ds(odd, LANES, stride=2), :] = sums[odd].T
    copy.wait()


def call(kernel, out_shape, specs, scratch=(), flops=0, limit=16, outs="v"):
    spaces = {"s": pltpu.SMEM, "v": pltpu.VMEM, "h": pltpu.HBM}
    out_specs = [pl.BlockSpec(memory_space=spaces[spec]) for spec in outs]
    if len(outs) == 1:
        out_specs = out_specs[0]
    return pl.pallas_call(
        kernel,
        out_shape=out_shape,
        in_specs=[pl.BlockSpec(memory_space=spaces[spec]) for spec in specs],
        out_specs=out_specs,
        scratch_shapes=list(scratch),
        compiler_params=pltpu.CompilerParams(vmem_limit_bytes=limit * MIB),
        cost_estimate=pl.CostEstimate(flops=flops, bytes_accessed=4 * MIB, transcendentals=0),
    )


def struct(shape, kind=F32):
    return jax.ShapeDtypeStruct(tuple(shape), kind)


def segment_transform(devices, place, samples):
    points = samples.size // 2
    return call(
        functools.partial(segment_kernel, devices),
        struct((points * 2 // LANES, LANES)),
        "sv",
        [
            pltpu.VMEM((2, 4, 2 * LANES, 2 * LANES), BF16),
            pltpu.VMEM((2, 4, 2 * LANES, SIDE), BF16),
            pltpu.VMEM((2, 4, SIDE, 2 * LANES), BF16),
        ],
        3 * 2 * 8 * SIDE * SIDE * LANES,
    )(place, samples)


def device_transform(devices, received):
    return call(
        functools.partial(device_kernel, devices),
        struct((ROWS * devices, LANES)),
        "vv",
        flops=3 * 2 * 2 * devices * received.shape[0] // 2 * LANES,
    )(received, jnp.asarray(device_table(devices)))


def gram_tables(index, offset):
    square = (2, LANES, LANES)
    return call(
        gram_tables_kernel,
        (
            struct(square, jnp.int32),
            struct((KEPT,) + square),
            struct((HALF + 3 - KEPT, 8, LANES)),
        ),
        "vv",
        flops=1 << 26,
        outs="vvv",
    )(index, offset)


def times_block(devices, place, timed, tables):
    rows = SIDE * SIDE // LANES
    return call(
        functools.partial(times_kernel, devices),
        (struct((rows, LANES)), struct((2 * LANES, LANES))),
        "svvvv",
        [
            pltpu.VMEM((4, SIDE + 2 * HALF, LANES), F32),
            pltpu.VMEM((rows, LANES), F32),
            pltpu.VMEM((2, 2 * HALF, LANES), F32),
            pltpu.VMEM((2, LANES, LANES), F32),
            pltpu.SemaphoreType.DMA(()),
        ],
        1 << 24,
        outs="hv",
    )(place, timed, *tables)


def local(samples, gram_index, gram_offset):
    inner, outer = lax.axis_size("inner"), lax.axis_size("outer")
    devices = inner * outer
    place = (lax.axis_index("inner") * outer + lax.axis_index("outer")).astype(jnp.int32)
    spot = place.reshape(1)
    points = samples.shape[2]
    parts = segment_transform(devices, spot, samples.reshape(2, points // LANES, LANES))
    received = lax.all_to_all(parts.reshape(devices, 16, LANES), AXES, 0, 0, tiled=True)
    real = device_transform(devices, received.reshape(16 * devices, LANES))
    rows = gram_index.shape[0] // LANES
    real, index, offset = lax.optimization_barrier(
        (real, gram_index.reshape(rows, LANES), gram_offset.reshape(rows, LANES))
    )
    timed = lax.all_to_all(real.reshape(-1), AXES, 0, 0, tiled=True)
    tables = gram_tables(index, offset)
    z_field, gram = times_block(
        devices, spot, timed.reshape(ROWS * devices, LANES), tables
    )
    return z_field.reshape(points), gram.reshape(-1)


def solution(mesh):
    return jax.shard_map(
        local,
        mesh=mesh,
        in_specs=(P(None, AXES, None), P(AXES), P(AXES)),
        out_specs=(P(AXES), P(AXES)),
        check_vma=False,
    )
```

time: 125 us -> 121 us (0.968)
  Pallas kernels: 14.4 us -> 10.8 us
  waiting for transfers between devices: 29.9 us -> 32.9 us
  local copies, waits for them, and re-layouts: 4.13 us -> 1.6 us
    all_to_all x1, waiting for transfers between devices: 29.9 us -> 32.9 us  [local(): timed = lax.all_to_all(real.reshape(-1), AXES, 0, 0, tiled=True)]
    pallas_call x1, Pallas kernels: 7.04 us -> 4.15 us  [segment_transform(): call(functools.partial(segment_kernel, devices), struct((points * 2 // LA...]
    unnamed x10 -> x8, local copies, waits for them, and re-layouts: 4.13 us -> 1.6 us
where the time goes in v3:
time: 121 us
  blocking collectives  67.8 us (56%)
  waiting for transfers between devices  32.9 us (27%)
  Pallas kernels  10.8 us (9%)
  starting transfers between devices  7.26 us (6%)
  local copies, waits for them, and re-layouts  1.6 us (1%)
    all_to_all x1, blocking collectives, local(): lax.all_to_all(parts.reshape(devices, 16, LANES), AXES, 0, 0, tiled=True)  67.8 us
    all_to_all x1, waiting for transfers between devices, local(): timed = lax.all_to_all(real.reshape(-1), AXES, 0, 0, tiled=True)  32.9 us
    all_to_all x1, starting transfers between devices, local(): timed = lax.all_to_all(real.reshape(-1), AXES, 0, 0, tiled=True)  7.26 us
    pallas_call x1, Pallas kernels, segment_transform(): call(functools.partial(segment_kernel, devices), struct((points * 2 // LA...  4.15 us
    pallas_call x1, Pallas kernels, times_block(): call(functools.partial(times_kernel, devices), (struct((rows, LANES)), st...  3.25 us
    pallas_call x1, Pallas kernels, device_transform(): call(functools.partial(device_kernel, devices), struct((ROWS * devices, L...  2.59 us
  transfers between devices with their start and end apart: 1, of which 1 were waited for; matrix products, arithmetic and copies ran while one was open for 0% of the time, Pallas kernels for 1%

profile of v3, /device:TPU:1, one launch (start us, length us, event | category | flops | bytes accessed | tf_op | source)
XLA Modules:
  0.0 121.0 jit_solution(1743474548906892831)
XLA Ops:
  0.6 0.0 copy-start.3
  0.6 1.6 %copy-done.3 = f32[2,1,262144]{2,1,0:T(1,128)S(1)} copy-done((f32[2,1,262144]{2,1,0:T(1,128)S(1)}, f32[2,1,262144]{2,1,0:T(1,128)}, u32[]{:S(2)}) %copy-start.3) | copy-done | bytes 2097176
  2.2 4.1 %shard_map.59 = f32[4096,128]{1,0:T(8,128)S(1)} custom-call(s32[1]{0:T(128)} %bitcast.place_ref, f32[2,2048,128]{2,1,0:T(8,128)S(1)} %bitcast.15), custom_call_target="tpu_custom_call" | custom-call | flops 1610612736 | bytes 4194304 | tf_op jit(solution)/shard_map/pallas_call | solution.py:312
  6.4 0.0 copy-start
  6.4 67.8 %all_to_all.14 = f32[256,16,128]{2,1,0:T(8,128)S(1)} all-to-all(f32[256,16,128]{2,1,0:T(8,128)S(1)} %bitcast.12), channel_id=1, replica_groups=mesh['inner'=32,'outer'=8] {'inner','outer'}, dimensions={0} | all-to-all | bytes 4194304 | tf_op jit(solution)/shard_map/all_to_all | solution.py:374
  74.2 0.0 copy-done
  74.2 2.6 %shard_map.60 = f32[2304,128]{1,0:T(8,128)} custom-call(f32[4096,128]{1,0:T(8,128)S(1)} %bitcast.10, bf16[2,256,512]{2,1,0:T(8,128)(2,1)S(1)} %copy-done), custom_call_target="tpu_custom_call" | custom-call | flops 805306368 | bytes 4194304 | tf_op jit(solution)/shard_map/pallas_call | solution.py:326
  76.8 0.0 copy-start.1
  76.8 0.0 copy-start.2
  76.8 7.3 %all-to-all-start.1 = ((f32[256,1152,1]{1,2,0:T(1,128)}), f32[256,1152,1]{1,2,0:T(1,128)S(1)}, u32[]{:S(2)}, u32[]{:S(2)}) async-start(f32[256,1152,1]{1,2,0:T(1,128)} %bitcast.6), calls=%async_computation.1 | async-start | bytes 2359296 | tf_op jit(solution)/shard_map/all_to_all | solution.py:380
  84.1 0.0 copy-done.1
  84.1 0.0 copy-done.2
  84.1 0.8 shard_map.61
  84.9 32.9 %all-to-all-done.1 = f32[256,1152,1]{1,2,0:T(1,128)S(1)} async-done(((f32[256,1152,1]{1,2,0:T(1,128)}), f32[256,1152,1]{1,2,0:T(1,128)S(1)}, u32[]{:S(2)}, u32[]{:S(2)}) %all-to-all-start.1) | async-done | bytes 1179680 | tf_op jit(solution)/shard_map/all_to_all | solution.py:380
  117.8 3.2 %shard_map.62 = (f32[2048,128]{1,0:T(8,128)}, f32[256,128]{1,0:T(8,128)}) custom-call(s32[1]{0:T(128)} %bitcast.place_ref, f32[2304,128]{1,0:T(8,128)S(1)} %bitcast.11, s32[2,128,128]{2,1,0:T(8,128)S(1)} %get-tuple-element.13.code_ref, f32[13,2,128,128]{3,2,1,0:T(8,128)S(1)} %get-tuple-element.14.share_ref, f32[6,8,128]{2,1,0:T(8,128)S(1)} %get-tuple-element.15.entry_ref), custom_call_target="tpu_custom_call" | custom-call | flops 16777216 | bytes 4194304 | tf_op jit(solution)/shard_map/pallas_call | solution.py:351
Async XLA Ops:
  0.6 1.6 %copy-start.3 = (f32[2,1,262144]{2,1,0:T(1,128)S(1)}, f32[2,1,262144]{2,1,0:T(1,128)}, u32[]{:S(2)}) copy-start(f32[2,1,262144]{2,1,0:T(1,128)} %param.4) | copy-start | bytes 6291460
  6.4 67.8 %copy-start = (bf16[2,256,512]{2,1,0:T(8,128)(2,1)S(1)}, bf16[2,256,512]{2,1,0:T(8,128)(2,1)}, u32[]{:S(2)}) copy-start(bf16[2,256,512]{2,1,0:T(8,128)(2,1)} %constant.13.clone.table_ref) | copy-start | bytes 1572868
  76.8 7.3 %copy-start.1 = (s32[32768]{0:T(1024)S(1)}, s32[32768]{0:T(1024)}, u32[]{:S(2)}) copy-start(s32[32768]{0:T(1024)} %param.5) | copy-start | bytes 393220
  76.8 7.3 %copy-start.2 = (s32[32768]{0:T(1024)S(1)}, s32[32768]{0:T(1024)}, u32[]{:S(2)}) copy-start(s32[32768]{0:T(1024)} %param.6) | copy-start | bytes 393220
  76.8 41.0 %all-to-all-start.1 = ((f32[256,1152,1]{1,2,0:T(1,128)}), f32[256,1152,1]{1,2,0:T(1,128)S(1)}, u32[]{:S(2)}, u32[]{:S(2)}) async-start(f32[256,1152,1]{1,2,0:T(1,128)} %bitcast.6), calls=%async_computation.1 | async-start | bytes 2359296 | tf_op jit(solution)/shard_map/all_to_all | solution.py:380

commit v4 on v3

--- a/solution.py
+++ b/solution.py
@@ -77,13 +77,15 @@
     return cosine, -sine
 
 
-def segment_kernel(devices, place_ref, x_ref, out_ref, table_ref, first_ref, second_ref):
+def segment_tables_kernel(devices, place_ref, table_ref, twiddle_ref, turn_ref):
     place = place_ref[0]
     points = SIDE * SIDE
     row = lax.broadcasted_iota(jnp.int32, (LANES, LANES), 0)
     lane = lax.broadcasted_iota(jnp.int32, (LANES, LANES), 1)
     line = lax.broadcasted_iota(jnp.int32, (8, LANES), 1)
     whole = unit(row * lane, LANES)
+    across = unit(row * lane, points // 4)
+    down = unit(row, SIDE)
     for g in range(4):
         here = whole
         if g:
@@ -94,6 +96,23 @@
             table_ref[k, g, :LANES, LANES:] = sin
             table_ref[k, g, LANES:, :LANES] = -sin
             table_ref[k, g, LANES:, LANES:] = cos
+        both = times(across, unit(place * (4 * row + g), points * devices))
+        step = down
+        if g:
+            both = times(both, tuple(x[:1] for x in unit(line * g, points)))
+            angle = -2.0 * math.pi * g * LANES / points
+            step = times(down, (math.cos(angle), math.sin(angle)))
+        for j in range(4):
+            if j:
+                both = times(both, step)
+            for part in range(2):
+                twiddle_ref[part, g, j] = both[part]
+        turn = unit(place * (4 * line + g), SIDE * devices)
+        for part in range(2):
+            turn_ref[part, g] = turn[part]
+
+
+def segment_kernel(x_ref, table_ref, twiddle_ref, turn_ref, out_ref, first_ref, second_ref):
     for j in range(4):
         grid = [
             tuple(x_ref[part, pl.ds(SIDE * i + j, LANES, stride=4), :] for part in range(2))
@@ -105,21 +124,12 @@
                 rows, cols = pl.ds(LANES * part, LANES), pl.ds(LANES * j, LANES)
                 first_ref[0, g, rows, cols] = high
                 first_ref[1, g, rows, cols] = low
-    across = unit(row * lane, points // 4)
-    down = unit(row, SIDE)
     for g in range(4):
         done = dot3((table_ref[0, g], table_ref[1, g]), (first_ref[0, g], first_ref[1, g]))
-        both = times(across, unit(place * (4 * row + g), points * devices))
-        step = down
-        if g:
-            both = times(both, tuple(x[:1] for x in unit(line * g, points)))
-            angle = -2.0 * math.pi * g * LANES / points
-            step = times(down, (math.cos(angle), math.sin(angle)))
         grid = []
         for j in range(4):
             cols = slice(LANES * j, LANES * (j + 1))
-            if j:
-                both = times(both, step)
+            both = (twiddle_ref[0, g, j], twiddle_ref[1, g, j])
             grid.append(times((done[:LANES, cols], done[LANES:, cols]), both))
         for h, pair in enumerate(quarter(grid)):
             for part in range(2):
@@ -131,8 +141,7 @@
         done = dot3(
             (second_ref[0, h], second_ref[1, h]), (table_ref[0, h], table_ref[1, h]), ((1,), (1,))
         )
-        turn = tuple(x[:1] for x in unit(place * (4 * line + h), SIDE * devices))
-        pair = times((done[:, :LANES], done[:, LANES:]), turn)
+        pair = times((done[:, :LANES], done[:, LANES:]), (turn_ref[0, h, :1], turn_ref[1, h, :1]))
         for part in range(2):
             for upper in range(2):
                 out_ref[pl.ds(8 * part + 4 * upper + h, SIDE // 2, stride=16), :] = pair[part][
@@ -307,19 +316,32 @@
     return jax.ShapeDtypeStruct(tuple(shape), kind)
 
 
-def segment_transform(devices, place, samples):
+def segment_tables(devices, place):
+    return call(
+        functools.partial(segment_tables_kernel, devices),
+        (
+            struct((2, 4, 2 * LANES, 2 * LANES), BF16),
+            struct((2, 4, 4, LANES, LANES)),
+            struct((2, 4, 8, LANES)),
+        ),
+        "s",
+        flops=1 << 32,
+        outs="vvv",
+    )(place)
+
+
+def segment_transform(samples, tables):
     points = samples.size // 2
     return call(
-        functools.partial(segment_kernel, devices),
+        segment_kernel,
         struct((points * 2 // LANES, LANES)),
-        "sv",
+        "vvvv",
         [
-            pltpu.VMEM((2, 4, 2 * LANES, 2 * LANES), BF16),
             pltpu.VMEM((2, 4, 2 * LANES, SIDE), BF16),
             pltpu.VMEM((2, 4, SIDE, 2 * LANES), BF16),
         ],
         3 * 2 * 8 * SIDE * SIDE * LANES,
-    )(place, samples)
+    )(samples, *tables)
 
 
 def device_transform(devices, received):
@@ -370,17 +392,19 @@
     place = (lax.axis_index("inner") * outer + lax.axis_index("outer")).astype(jnp.int32)
     spot = place.reshape(1)
     points = samples.shape[2]
-    parts = segment_transform(devices, spot, samples.reshape(2, points // LANES, LANES))
+    rows = gram_index.shape[0] // LANES
+    tables = segment_tables(devices, spot)
+    tables, index, offset = lax.optimization_barrier(
+        (tables, gram_index.reshape(rows, LANES), gram_offset.reshape(rows, LANES))
+    )
+    weights = gram_tables(index, offset)
+    tables, weights = lax.optimization_barrier((tables, weights))
+    parts = segment_transform(samples.reshape(2, points // LANES, LANES), tables)
     received = lax.all_to_all(parts.reshape(devices, 16, LANES), AXES, 0, 0, tiled=True)
     real = device_transform(devices, received.reshape(16 * devices, LANES))
-    rows = gram_index.shape[0] // LANES
-    real, index, offset = lax.optimization_barrier(
-        (real, gram_index.reshape(rows, LANES), gram_offset.reshape(rows, LANES))
-    )
     timed = lax.all_to_all(real.reshape(-1), AXES, 0, 0, tiled=True)
-    tables = gram_tables(index, offset)
     z_field, gram = times_block(
-        devices, spot, timed.reshape(ROWS * devices, LANES), tables
+        devices, spot, timed.reshape(ROWS * devices, LANES), weights
     )
     return z_field.reshape(points), gram.reshape(-1)
 

time: 121 us -> 119 us (0.983)
  blocking collectives: 67.8 us -> 109 us
  waiting for transfers between devices: 32.9 us -> 0 us
  starting transfers between devices: 7.26 us -> 0 us
  local copies, waits for them, and re-layouts: 1.6 us -> 0.02 us
    all_to_all x0 -> x1, blocking collectives: none -> 40.8 us  [local(): timed = lax.all_to_all(real.reshape(-1), AXES, 0, 0, tiled=True)]
    all_to_all x1 -> x0, waiting for transfers between devices: 32.9 us -> none  [local(): timed = lax.all_to_all(real.reshape(-1), AXES, 0, 0, tiled=True)]
    all_to_all x1 -> x0, starting transfers between devices: 7.26 us -> none  [local(): timed = lax.all_to_all(real.reshape(-1), AXES, 0, 0, tiled=True)]
    unnamed x8, local copies, waits for them, and re-layouts: 1.6 us -> 0.02 us
    pallas_call x1 -> x2, Pallas kernels: 4.15 us -> 4.23 us  [the longest x1 3.03 us: segment_transform(): call(segment_kernel, struct((points * 2 // LANES, LANES)), 'vvvv', [pltpu...]
  transfers between devices with their start and end apart: 1 -> 0, of which waited for: 1 -> 0; matrix products, arithmetic and copies ran while one was open for 0% -> 0% of each run, Pallas kernels for 1% -> 0%
where the time goes in v4:
time: 119 us
  blocking collectives  109 us (92%)
  Pallas kernels  9.81 us (8%)
    all_to_all x1, blocking collectives, local(): lax.all_to_all(parts.reshape(devices, 16, LANES), AXES, 0, 0, tiled=True)  67.8 us
    all_to_all x1, blocking collectives, local(): timed = lax.all_to_all(real.reshape(-1), AXES, 0, 0, tiled=True)  40.8 us
    pallas_call x1, Pallas kernels, times_block(): call(functools.partial(times_kernel, devices), (struct((rows, LANES)), st...  3.25 us
    pallas_call x1, Pallas kernels, segment_transform(): call(segment_kernel, struct((points * 2 // LANES, LANES)), 'vvvv', [pltpu...  3.03 us

profile of v4, /device:TPU:1, one launch (start us, length us, event | category | flops | bytes accessed | tf_op | source)
XLA Modules:
  0.0 119.2 jit_solution(12008214620389286580)
XLA Ops:
  0.6 0.0 copy-start.2
  0.6 0.0 copy-start.3
  0.7 0.0 copy-start
  0.7 1.2 %shard_map.59 = (bf16[2,4,256,256]{3,2,1,0:T(8,128)(2,1)S(1)}, f32[2,4,4,128,128]{4,3,2,1,0:T(8,128)S(1)}, f32[2,4,8,128]{3,2,1,0:T(8,128)S(1)}) custom-call(s32[1]{0:T(128)} %bitcast.place_ref), custom_call_target="tpu_custom_call" | custom-call | flops 4294967296 | bytes 4194304 | tf_op jit(solution)/shard_map/pallas_call | solution.py:320
  1.9 0.0 copy-done.2
  1.9 0.0 copy-done.3
  1.9 0.8 shard_map.60
  2.7 0.0 copy-done
  2.7 3.0 %shard_map.61 = f32[4096,128]{1,0:T(8,128)S(1)} custom-call(f32[2,2048,128]{2,1,0:T(8,128)S(1)} %bitcast.14, bf16[2,4,256,256]{3,2,1,0:T(8,128)(2,1)S(1)} %get-tuple-element.32.table_ref, f32[2,4,4,128,128]{4,3,2,1,0:T(8,128)S(1)} %get-tuple-element.33.twiddle_ref, f32[2,4,8,128]{3,2,1,0:T(8,128)S(1)} %get-tuple-element.34.turn_ref), custom_call_target="tpu_custom_call" | custom-call | flops 1610612736 | bytes 4194304 | tf_op jit(solution)/shard_map/pallas_call | solution.py:335
  5.8 0.0 copy-start.1
  5.8 67.8 %all_to_all.14 = f32[256,16,128]{2,1,0:T(8,128)S(1)} all-to-all(f32[256,16,128]{2,1,0:T(8,128)S(1)} %bitcast.10), channel_id=1, replica_groups=mesh['inner'=32,'outer'=8] {'inner','outer'}, dimensions={0} | all-to-all | bytes 4194304 | tf_op jit(solution)/shard_map/all_to_all | solution.py:403
  73.6 0.0 copy-done.1
  73.6 1.5 %shard_map.62 = f32[2304,128]{1,0:T(8,128)S(1)} custom-call(f32[4096,128]{1,0:T(8,128)S(1)} %bitcast.11, bf16[2,256,512]{2,1,0:T(8,128)(2,1)S(1)} %copy-done.1), custom_call_target="tpu_custom_call" | custom-call | flops 805306368 | bytes 4194304 | tf_op jit(solution)/shard_map/pallas_call | solution.py:348
  75.1 40.8 %all_to_all.15 = f32[256,1152,1]{1,2,0:T(1,128)S(1)} all-to-all(f32[256,1152,1]{1,2,0:T(1,128)S(1)} %bitcast.13), channel_id=1, replica_groups=mesh['inner'=32,'outer'=8] {'inner','outer'}, dimensions={0} | all-to-all | bytes 2359296 | tf_op jit(solution)/shard_map/all_to_all | solution.py:405
  115.9 3.3 %shard_map.63 = (f32[2048,128]{1,0:T(8,128)}, f32[256,128]{1,0:T(8,128)}) custom-call(s32[1]{0:T(128)} %bitcast.place_ref, f32[2304,128]{1,0:T(8,128)S(1)} %bitcast.12, s32[2,128,128]{2,1,0:T(8,128)S(1)} %get-tuple-element.35.code_ref, f32[13,2,128,128]{3,2,1,0:T(8,128)S(1)} %get-tuple-element.36.share_ref, f32[6,8,128]{2,1,0:T(8,128)S(1)} %get-tuple-element.37.entry_ref), custom_call_target="tpu_custom_call" | custom-call | flops 16777216 | bytes 4194304 | tf_op jit(solution)/shard_map/pallas_call | solution.py:373
Async XLA Ops:
  0.6 1.2 %copy-start.2 = (s32[32768]{0:T(1024)S(1)}, s32[32768]{0:T(1024)}, u32[]{:S(2)}) copy-start(s32[32768]{0:T(1024)} %param.5) | copy-start | bytes 393220
  0.6 1.2 %copy-start.3 = (s32[32768]{0:T(1024)S(1)}, s32[32768]{0:T(1024)}, u32[]{:S(2)}) copy-start(s32[32768]{0:T(1024)} %param.6) | copy-start | bytes 393220
  0.7 2.1 %copy-start = (f32[2,1,262144]{2,1,0:T(1,128)S(1)}, f32[2,1,262144]{2,1,0:T(1,128)}, u32[]{:S(2)}) copy-start(f32[2,1,262144]{2,1,0:T(1,128)} %param.4) | copy-start | bytes 6291460
  5.8 67.8 %copy-start.1 = (bf16[2,256,512]{2,1,0:T(8,128)(2,1)S(1)}, bf16[2,256,512]{2,1,0:T(8,128)(2,1)}, u32[]{:S(2)}) copy-start(bf16[2,256,512]{2,1,0:T(8,128)(2,1)} %constant.13.clone.table_ref) | copy-start | bytes 1572868

commit v5 on v4

--- a/solution.py
+++ b/solution.py
@@ -84,7 +84,7 @@
     lane = lax.broadcasted_iota(jnp.int32, (LANES, LANES), 1)
     line = lax.broadcasted_iota(jnp.int32, (8, LANES), 1)
     whole = unit(row * lane, LANES)
-    across = unit(row * lane, points // 4)
+    across = times(unit(row * lane, points // 4), unit(place * row * 4, points * devices))
     down = unit(row, SIDE)
     for g in range(4):
         here = whole
@@ -96,10 +96,11 @@
             table_ref[k, g, :LANES, LANES:] = sin
             table_ref[k, g, LANES:, :LANES] = -sin
             table_ref[k, g, LANES:, LANES:] = cos
-        both = times(across, unit(place * (4 * row + g), points * devices))
+        both = across
         step = down
         if g:
-            both = times(both, tuple(x[:1] for x in unit(line * g, points)))
+            part_g = times(unit(line * g, points), unit(place * g + 0 * line, points * devices))
+            both = times(both, tuple(x[:1] for x in part_g))
             angle = -2.0 * math.pi * g * LANES / points
             step = times(down, (math.cos(angle), math.sin(angle)))
         for j in range(4):
@@ -200,32 +201,36 @@
     at_zero = fraction == 0.0
     shares = [jnp.where(at_zero, 1.0, sine / jnp.where(at_zero, 1.0, fraction))]
     square = fraction * fraction
-    for w in range(1, HALF + 1):
-        scale = (-1.0) ** w * math.exp(-0.5 * w * w / (SPREAD * SPREAD))
-        shares.append(sine * (scale / (square - w * w)))
-    shares.append(jnp.exp(fraction * (1.0 / (SPREAD * SPREAD))))
-    shares.append(jnp.exp(fraction * (-1.0 / (SPREAD * SPREAD))))
+    up = jnp.exp(fraction * (1.0 / (SPREAD * SPREAD)))
+    for w in range(1, HALF, 2):
+        odd, even = square - w * w, square - (w + 1) * (w + 1)
+        inverse = 1.0 / (odd * even)
+        for tap, other in ((w, even), (w + 1, odd)):
+            scale = (-1.0) ** tap * math.exp(-0.5 * tap * tap / (SPREAD * SPREAD))
+            sine = sine * up
+            shares.append((sine * scale) * (other * inverse))
+    shares.append(jnp.exp(fraction * (-2.0 / (SPREAD * SPREAD))))
     return shares
 
 
 def weighted(taps, shares, fraction):
-    up, down = shares[HALF + 1], shares[HALF + 2]
-    ups, downs = up, down
+    down = shares[HALF + 1]
+    downs = down
     terms = [taps[HALF - 1] * shares[0]]
     for w in range(1, HALF + 1):
-        term = (ups * taps[HALF - 1 + w]) * (fraction + w)
+        term = taps[HALF - 1 + w] * (fraction + w)
         if w < HALF:
             term = term + (downs * taps[HALF - 1 - w]) * (fraction - w)
         terms.append(term * shares[w])
-        ups, downs = ups * up, downs * down
+        downs = downs * down
     while len(terms) > 1:
         terms = [a + b for a, b in zip(terms[::2], terms[1::2])] + terms[len(terms) & ~1 :]
     return terms[0]
 
 
 def times_kernel(
-    devices, place_ref, x_ref, code_ref, share_ref, entry_ref, z_hbm, gram_ref,
-    zs_ref, z_ref, ends_ref, sums, sem,
+    devices, place_ref, x_ref, code_ref, share_ref, entry_ref, z_hbm, gram_hbm,
+    zs_ref, z_ref, ends_ref, sums, gram_ref, sem, gram_sem,
 ):
     pad = HALF
     place = place_ref[0]
@@ -285,7 +290,7 @@
                 chosen = (index >> bit & 1) == 1
                 taps = [jnp.where(chosen, b, a) for a, b in zip(taps[:-size], taps[size:])]
             shares = [share_ref[w, h // 2, rows, :] for w in range(KEPT)]
-            for w in range(HALF + 3 - KEPT):
+            for w in range(HALF + 2 - KEPT):
                 shares.append(jnp.take_along_axis(entry_ref[w], offset, axis=1))
             sums[h // 2, rows, :] = weighted(taps, shares, fraction)
             return carry
@@ -293,7 +298,10 @@
         lax.fori_loop(0, 8, body, 0, unroll=4)
     for odd in range(2):
         gram_ref[pl.ds(odd, LANES, stride=2), :] = sums[odd].T
+    gram_copy = pltpu.make_async_copy(gram_ref, gram_hbm, gram_sem)
+    gram_copy.start()
     copy.wait()
+    gram_copy.wait()
 
 
 def call(kernel, out_shape, specs, scratch=(), flops=0, limit=16, outs="v"):
@@ -360,7 +368,7 @@
         (
             struct(square, jnp.int32),
             struct((KEPT,) + square),
-            struct((HALF + 3 - KEPT, 8, LANES)),
+            struct((HALF + 2 - KEPT, 8, LANES)),
         ),
         "vv",
         flops=1 << 26,
@@ -379,10 +387,12 @@
             pltpu.VMEM((rows, LANES), F32),
             pltpu.VMEM((2, 2 * HALF, LANES), F32),
             pltpu.VMEM((2, LANES, LANES), F32),
+            pltpu.VMEM((2 * LANES, LANES), F32),
+            pltpu.SemaphoreType.DMA(()),
             pltpu.SemaphoreType.DMA(()),
         ],
         1 << 24,
-        outs="hv",
+        outs="hh",
     )(place, timed, *tables)
 
 

time: 119 us -> 119 us (level)
  no operation moved by 1% of the time
where the time goes in v5:
time: 119 us
  blocking collectives  109 us (92%)
  Pallas kernels  9.52 us (8%)
    all_to_all x1, blocking collectives, local(): lax.all_to_all(parts.reshape(devices, 16, LANES), AXES, 0, 0, tiled=True)  67.8 us
    all_to_all x1, blocking collectives, local(): timed = lax.all_to_all(real.reshape(-1), AXES, 0, 0, tiled=True)  40.8 us
    pallas_call x1, Pallas kernels, times_block(): call(functools.partial(times_kernel, devices), (struct((rows, LANES)), st...  3.05 us
    pallas_call x1, Pallas kernels, segment_transform(): call(segment_kernel, struct((points * 2 // LANES, LANES)), 'vvvv', [pltpu...  3.03 us

profile of v5, /device:TPU:1, one launch (start us, length us, event | category | flops | bytes accessed | tf_op | source)
XLA Modules:
  0.0 118.9 jit_solution(1794175243992862945)
XLA Ops:
  0.6 0.0 copy-start.2
  0.6 0.0 copy-start.3
  0.7 0.0 copy-start
  0.7 0.9 shard_map.59
  1.6 0.0 copy-done.2
  1.6 0.0 copy-done.3
  1.6 1.0 shard_map.60
  2.6 0.0 copy-done
  2.6 3.0 %shard_map.61 = f32[4096,128]{1,0:T(8,128)S(1)} custom-call(f32[2,2048,128]{2,1,0:T(8,128)S(1)} %bitcast.14, bf16[2,4,256,256]{3,2,1,0:T(8,128)(2,1)S(1)} %get-tuple-element.32.table_ref, f32[2,4,4,128,128]{4,3,2,1,0:T(8,128)S(1)} %get-tuple-element.33.twiddle_ref, f32[2,4,8,128]{3,2,1,0:T(8,128)S(1)} %get-tuple-element.34.turn_ref), custom_call_target="tpu_custom_call" | custom-call | flops 1610612736 | bytes 4194304 | tf_op jit(solution)/shard_map/pallas_call | solution.py:343
  5.7 0.0 copy-start.1
  5.7 67.8 %all_to_all.14 = f32[256,16,128]{2,1,0:T(8,128)S(1)} all-to-all(f32[256,16,128]{2,1,0:T(8,128)S(1)} %bitcast.10), channel_id=1, replica_groups=mesh['inner'=32,'outer'=8] {'inner','outer'}, dimensions={0} | all-to-all | bytes 4194304 | tf_op jit(solution)/shard_map/all_to_all | solution.py:413
  73.5 0.0 copy-done.1
  73.5 1.5 %shard_map.62 = f32[2304,128]{1,0:T(8,128)S(1)} custom-call(f32[4096,128]{1,0:T(8,128)S(1)} %bitcast.11, bf16[2,256,512]{2,1,0:T(8,128)(2,1)S(1)} %copy-done.1), custom_call_target="tpu_custom_call" | custom-call | flops 805306368 | bytes 4194304 | tf_op jit(solution)/shard_map/pallas_call | solution.py:356
  75.0 40.8 %all_to_all.15 = f32[256,1152,1]{1,2,0:T(1,128)S(1)} all-to-all(f32[256,1152,1]{1,2,0:T(1,128)S(1)} %bitcast.13), channel_id=1, replica_groups=mesh['inner'=32,'outer'=8] {'inner','outer'}, dimensions={0} | all-to-all | bytes 2359296 | tf_op jit(solution)/shard_map/all_to_all | solution.py:415
  115.8 3.0 %shard_map.63 = (f32[2048,128]{1,0:T(8,128)}, f32[256,128]{1,0:T(8,128)}) custom-call(s32[1]{0:T(128)} %bitcast.place_ref, f32[2304,128]{1,0:T(8,128)S(1)} %bitcast.12, s32[2,128,128]{2,1,0:T(8,128)S(1)} %get-tuple-element.35.code_ref, f32[13,2,128,128]{3,2,1,0:T(8,128)S(1)} %get-tuple-element.36.share_ref, f32[5,8,128]{2,1,0:T(8,128)S(1)} %get-tuple-element.37.entry_ref), custom_call_target="tpu_custom_call" | custom-call | flops 16777216 | bytes 4194304 | tf_op jit(solution)/shard_map/pallas_call | solution.py:381
Async XLA Ops:
  0.6 0.9 copy-start.2
  0.6 1.0 copy-start.3
  0.7 2.0 %copy-start = (f32[2,1,262144]{2,1,0:T(1,128)S(1)}, f32[2,1,262144]{2,1,0:T(1,128)}, u32[]{:S(2)}) copy-start(f32[2,1,262144]{2,1,0:T(1,128)} %param.4) | copy-start | bytes 6291460
  5.7 67.8 %copy-start.1 = (bf16[2,256,512]{2,1,0:T(8,128)(2,1)S(1)}, bf16[2,256,512]{2,1,0:T(8,128)(2,1)}, u32[]{:S(2)}) copy-start(bf16[2,256,512]{2,1,0:T(8,128)(2,1)} %constant.13.clone.table_ref) | copy-start | bytes 1572868

commit v6 on v5

--- a/solution.py
+++ b/solution.py
@@ -31,9 +31,12 @@
 
 
 def device_table(devices):
-    n = np.arange(devices)
-    angle = 2.0 * np.pi * (n[:, None] * n[None, :] % devices) / devices
-    return halves(np.concatenate([np.cos(angle), np.sin(angle)], axis=1))
+    n = np.arange(devices // 2)
+    tables = []
+    for g in range(2):
+        angle = 2.0 * np.pi * ((2 * n[:, None] + g) * n[None, :] % devices) / devices
+        tables.append(np.concatenate([np.cos(angle), np.sin(angle)], axis=1))
+    return halves(np.stack(tables))
 
 
 def split(x):
@@ -151,29 +154,37 @@
 
 
 def device_kernel(devices, x_ref, table_ref, out_ref):
+    count = devices // 2
     edges = {}
     for block in range(4):
-        columns = []
+        columns = ([], [])
         for e in (2 * block, 2 * block + 1):
-            columns.append(
-                jnp.concatenate(
-                    [x_ref[pl.ds(8 * part + e, devices, stride=16), :] for part in range(2)], axis=0
-                )
-            )
-        x = jnp.concatenate(columns, axis=1)
-        done = dot3((table_ref[0], table_ref[1]), split(x))
-        for i, e in enumerate((2 * block, 2 * block + 1)):
-            values = done[:, LANES * i : LANES * (i + 1)]
-            out_ref[pl.ds(e, devices, stride=ROWS), :] = values
-            if e % 4 in (0, 3):
-                edges[e] = values
-    lane = lax.broadcasted_iota(jnp.int32, (devices, LANES), 1)
-    row = lax.broadcasted_iota(jnp.int32, (devices, LANES), 0)
-    after = jnp.where(lane == 0, edges[0], pltpu.roll(edges[4], 1, 1))
-    before = jnp.where(lane == LANES - 1, edges[3], pltpu.roll(edges[7], LANES - 1, 1))
-    after = jnp.where(row == devices - 1, 0.0, pltpu.roll(after, devices - 1, 0))
-    before = jnp.where(row == 0, 0.0, pltpu.roll(before, 1, 0))
-    out_ref[pl.ds(8, devices, stride=ROWS), :] = jnp.where(lane < 2, after, before)
+            pairs = [
+                [x_ref[pl.ds(16 * count * i + 8 * part + e, count, stride=16), :] for i in range(2)]
+                for part in range(2)
+            ]
+            columns[0].append(jnp.concatenate([low + high for low, high in pairs], axis=0))
+            columns[1].append(jnp.concatenate([low - high for low, high in pairs], axis=0))
+        for g in range(2):
+            x = jnp.concatenate(columns[g], axis=1)
+            done = dot3((table_ref[0, g], table_ref[1, g]), split(x))
+            for i, e in enumerate((2 * block, 2 * block + 1)):
+                values = done[:, LANES * i : LANES * (i + 1)]
+                out_ref[pl.ds(ROWS * g + e, count, stride=2 * ROWS), :] = values
+                if e % 4 in (0, 3):
+                    edges[e, g] = values
+    lane = lax.broadcasted_iota(jnp.int32, (count, LANES), 1)
+    row = lax.broadcasted_iota(jnp.int32, (count, LANES), 0)
+    after, before = [], []
+    for g in range(2):
+        after.append(jnp.where(lane == 0, edges[0, g], pltpu.roll(edges[4, g], 1, 1)))
+        before.append(
+            jnp.where(lane == LANES - 1, edges[3, g], pltpu.roll(edges[7, g], LANES - 1, 1))
+        )
+    later = jnp.where(row == count - 1, 0.0, pltpu.roll(after[0], count - 1, 0))
+    earlier = jnp.where(row == 0, 0.0, pltpu.roll(before[1], 1, 0))
+    for g, (up, down) in enumerate(((after[1], earlier), (later, before[0]))):
+        out_ref[pl.ds(ROWS * g + 8, count, stride=2 * ROWS), :] = jnp.where(lane < 2, up, down)
 
 
 def gain(devices, place, position):

time: 119 us -> 119 us (level)
  no operation moved by 1% of the time
where the time goes in v6:
time: 119 us
  blocking collectives  109 us (92%)
  Pallas kernels  9.34 us (8%)
    all_to_all x1, blocking collectives, local(): lax.all_to_all(parts.reshape(devices, 16, LANES), AXES, 0, 0, tiled=True)  67.8 us
    all_to_all x1, blocking collectives, local(): timed = lax.all_to_all(real.reshape(-1), AXES, 0, 0, tiled=True)  40.8 us
    pallas_call x1, Pallas kernels, times_block(): call(functools.partial(times_kernel, devices), (struct((rows, LANES)), st...  3.05 us
    pallas_call x1, Pallas kernels, segment_transform(): call(segment_kernel, struct((points * 2 // LANES, LANES)), 'vvvv', [pltpu...  3.03 us

profile of v6, /device:TPU:1, one launch (start us, length us, event | category | flops | bytes accessed | tf_op | source)
XLA Modules:
  0.0 118.7 jit_solution(13579184911093663813)
XLA Ops:
  0.6 0.0 copy-start.2
  0.6 0.0 copy-start.3
  0.7 0.0 copy-start
  0.7 0.9 shard_map.59
  1.6 0.0 copy-done.2
  1.6 0.0 copy-done.3
  1.6 1.0 shard_map.60
  2.6 0.0 copy-done
  2.6 3.0 %shard_map.61 = f32[4096,128]{1,0:T(8,128)S(1)} custom-call(f32[2,2048,128]{2,1,0:T(8,128)S(1)} %bitcast.14, bf16[2,4,256,256]{3,2,1,0:T(8,128)(2,1)S(1)} %get-tuple-element.32.table_ref, f32[2,4,4,128,128]{4,3,2,1,0:T(8,128)S(1)} %get-tuple-element.33.twiddle_ref, f32[2,4,8,128]{3,2,1,0:T(8,128)S(1)} %get-tuple-element.34.turn_ref), custom_call_target="tpu_custom_call" | custom-call | flops 1610612736 | bytes 4194304 | tf_op jit(solution)/shard_map/pallas_call | solution.py:354
  5.7 0.0 copy-start.1
  5.7 67.8 %all_to_all.14 = f32[256,16,128]{2,1,0:T(8,128)S(1)} all-to-all(f32[256,16,128]{2,1,0:T(8,128)S(1)} %bitcast.10), channel_id=1, replica_groups=mesh['inner'=32,'outer'=8] {'inner','outer'}, dimensions={0} | all-to-all | bytes 4194304 | tf_op jit(solution)/shard_map/all_to_all | solution.py:424
  73.5 0.0 copy-done.1
  73.5 1.3 %shard_map.62 = f32[2304,128]{1,0:T(8,128)S(1)} custom-call(f32[4096,128]{1,0:T(8,128)S(1)} %bitcast.11, bf16[2,2,128,256]{3,2,1,0:T(8,128)(2,1)S(1)} %copy-done.1), custom_call_target="tpu_custom_call" | custom-call | flops 805306368 | bytes 4194304 | tf_op jit(solution)/shard_map/pallas_call | solution.py:367
  74.8 40.8 %all_to_all.15 = f32[256,1152,1]{1,2,0:T(1,128)S(1)} all-to-all(f32[256,1152,1]{1,2,0:T(1,128)S(1)} %bitcast.12), channel_id=1, replica_groups=mesh['inner'=32,'outer'=8] {'inner','outer'}, dimensions={0} | all-to-all | bytes 2359296 | tf_op jit(solution)/shard_map/all_to_all | solution.py:426
  115.7 3.0 %shard_map.63 = (f32[2048,128]{1,0:T(8,128)}, f32[256,128]{1,0:T(8,128)}) custom-call(s32[1]{0:T(128)} %bitcast.place_ref, f32[2304,128]{1,0:T(8,128)S(1)} %bitcast.13, s32[2,128,128]{2,1,0:T(8,128)S(1)} %get-tuple-element.35.code_ref, f32[13,2,128,128]{3,2,1,0:T(8,128)S(1)} %get-tuple-element.36.share_ref, f32[5,8,128]{2,1,0:T(8,128)S(1)} %get-tuple-element.37.entry_ref), custom_call_target="tpu_custom_call" | custom-call | flops 16777216 | bytes 4194304 | tf_op jit(solution)/shard_map/pallas_call | solution.py:392
Async XLA Ops:
  0.6 0.9 copy-start.2
  0.6 1.0 copy-start.3
  0.7 2.0 %copy-start = (f32[2,1,262144]{2,1,0:T(1,128)S(1)}, f32[2,1,262144]{2,1,0:T(1,128)}, u32[]{:S(2)}) copy-start(f32[2,1,262144]{2,1,0:T(1,128)} %param.4) | copy-start | bytes 6291460
  5.7 67.8 %copy-start.1 = (bf16[2,2,128,256]{3,2,1,0:T(8,128)(2,1)S(1)}, bf16[2,2,128,256]{3,2,1,0:T(8,128)(2,1)}, u32[]{:S(2)}) copy-start(bf16[2,2,128,256]{3,2,1,0:T(8,128)(2,1)} %constant.13.clone.table_ref) | copy-start | bytes 786436

commit v7 on v6

--- a/solution.py
+++ b/solution.py
@@ -16,7 +16,7 @@
 SPREAD = HALF / 2.0
 SIDE = 512
 LANES = 128
-KEPT = 13
+KEPT = 9
 ROWS = 9
 AXES = ("inner", "outer")
 F32 = jnp.float32

time: 119 us -> 119 us (level)
  no operation moved by 1% of the time
where the time goes in v7:
time: 119 us
  blocking collectives  109 us (92%)
  Pallas kernels  9.2 us (8%)
    all_to_all x1, blocking collectives, local(): lax.all_to_all(parts.reshape(devices, 16, LANES), AXES, 0, 0, tiled=True)  67.8 us
    all_to_all x1, blocking collectives, local(): timed = lax.all_to_all(real.reshape(-1), AXES, 0, 0, tiled=True)  40.8 us
    pallas_call x1, Pallas kernels, segment_transform(): call(segment_kernel, struct((points * 2 // LANES, LANES)), 'vvvv', [pltpu...  3.03 us
    pallas_call x1, Pallas kernels, times_block(): call(functools.partial(times_kernel, devices), (struct((rows, LANES)), st...  3.02 us

profile of v7, /device:TPU:1, one launch (start us, length us, event | category | flops | bytes accessed | tf_op | source)
XLA Modules:
  0.0 118.5 jit_solution(10060464184068612750)
XLA Ops:
  0.6 0.0 copy-start.2
  0.6 0.0 copy-start.3
  0.7 0.0 copy-start
  0.7 0.9 shard_map.59
  1.6 0.0 copy-done.2
  1.6 0.0 copy-done.3
  1.6 0.9 shard_map.60
  2.5 0.0 copy-done
  2.5 3.0 %shard_map.61 = f32[4096,128]{1,0:T(8,128)S(1)} custom-call(f32[2,2048,128]{2,1,0:T(8,128)S(1)} %bitcast.14, bf16[2,4,256,256]{3,2,1,0:T(8,128)(2,1)S(1)} %get-tuple-element.32.table_ref, f32[2,4,4,128,128]{4,3,2,1,0:T(8,128)S(1)} %get-tuple-element.33.twiddle_ref, f32[2,4,8,128]{3,2,1,0:T(8,128)S(1)} %get-tuple-element.34.turn_ref), custom_call_target="tpu_custom_call" | custom-call | flops 1610612736 | bytes 4194304 | tf_op jit(solution)/shard_map/pallas_call | solution.py:354
  5.6 0.0 copy-start.1
  5.6 67.8 %all_to_all.14 = f32[256,16,128]{2,1,0:T(8,128)S(1)} all-to-all(f32[256,16,128]{2,1,0:T(8,128)S(1)} %bitcast.10), channel_id=1, replica_groups=mesh['inner'=32,'outer'=8] {'inner','outer'}, dimensions={0} | all-to-all | bytes 4194304 | tf_op jit(solution)/shard_map/all_to_all | solution.py:424
  73.4 0.0 copy-done.1
  73.4 1.3 %shard_map.62 = f32[2304,128]{1,0:T(8,128)S(1)} custom-call(f32[4096,128]{1,0:T(8,128)S(1)} %bitcast.11, bf16[2,2,128,256]{3,2,1,0:T(8,128)(2,1)S(1)} %copy-done.1), custom_call_target="tpu_custom_call" | custom-call | flops 805306368 | bytes 4194304 | tf_op jit(solution)/shard_map/pallas_call | solution.py:367
  74.7 40.8 %all_to_all.15 = f32[256,1152,1]{1,2,0:T(1,128)S(1)} all-to-all(f32[256,1152,1]{1,2,0:T(1,128)S(1)} %bitcast.12), channel_id=1, replica_groups=mesh['inner'=32,'outer'=8] {'inner','outer'}, dimensions={0} | all-to-all | bytes 2359296 | tf_op jit(solution)/shard_map/all_to_all | solution.py:426
  115.5 3.0 %shard_map.63 = (f32[2048,128]{1,0:T(8,128)}, f32[256,128]{1,0:T(8,128)}) custom-call(s32[1]{0:T(128)} %bitcast.place_ref, f32[2304,128]{1,0:T(8,128)S(1)} %bitcast.13, s32[2,128,128]{2,1,0:T(8,128)S(1)} %get-tuple-element.35.code_ref, f32[9,2,128,128]{3,2,1,0:T(8,128)S(1)} %get-tuple-element.36.share_ref, f32[9,8,128]{2,1,0:T(8,128)S(1)} %get-tuple-element.37.entry_ref), custom_call_target="tpu_custom_call" | custom-call | flops 16777216 | bytes 4194304 | tf_op jit(solution)/shard_map/pallas_call | solution.py:392
Async XLA Ops:
  0.6 0.9 copy-start.2
  0.6 1.0 copy-start.3
  0.7 1.9 %copy-start = (f32[2,1,262144]{2,1,0:T(1,128)S(1)}, f32[2,1,262144]{2,1,0:T(1,128)}, u32[]{:S(2)}) copy-start(f32[2,1,262144]{2,1,0:T(1,128)} %param.4) | copy-start | bytes 6291460
  5.6 67.8 %copy-start.1 = (bf16[2,2,128,256]{3,2,1,0:T(8,128)(2,1)S(1)}, bf16[2,2,128,256]{3,2,1,0:T(8,128)(2,1)}, u32[]{:S(2)}) copy-start(bf16[2,2,128,256]{3,2,1,0:T(8,128)(2,1)} %constant.13.clone.table_ref) | copy-start | bytes 786436

commit v8 on v7

--- a/solution.py
+++ b/solution.py
@@ -16,7 +16,7 @@
 SPREAD = HALF / 2.0
 SIDE = 512
 LANES = 128
-KEPT = 9
+KEPT = 5
 ROWS = 9
 AXES = ("inner", "outer")
 F32 = jnp.float32

time: 119 us -> 119 us (level)
  no operation moved by 1% of the time
where the time goes in v8:
time: 119 us; the launch traced here: 118 us
  blocking collectives  109 us (92%)
  Pallas kernels  9.13 us (8%)
    all_to_all x1, blocking collectives, local(): lax.all_to_all(parts.reshape(devices, 16, LANES), AXES, 0, 0, tiled=True)  67.8 us
    all_to_all x1, blocking collectives, local(): timed = lax.all_to_all(real.reshape(-1), AXES, 0, 0, tiled=True)  40.8 us
    pallas_call x1, Pallas kernels, segment_transform(): call(segment_kernel, struct((points * 2 // LANES, LANES)), 'vvvv', [pltpu...  3.07 us
    pallas_call x1, Pallas kernels, times_block(): call(functools.partial(times_kernel, devices), (struct((rows, LANES)), st...  3.04 us

profile of v8, /device:TPU:1, one launch (start us, length us, event | category | flops | bytes accessed | tf_op | source)
XLA Modules:
  0.0 118.5 jit_solution(4244862471867004647)
XLA Ops:
  0.6 0.0 copy-start.2
  0.6 0.0 copy-start.3
  0.7 0.0 copy-start
  0.7 0.9 shard_map.59
  1.6 0.0 copy-done.2
  1.6 0.0 copy-done.3
  1.6 0.8 shard_map.60
  2.4 0.0 copy-done
  2.4 3.1 %shard_map.61 = f32[4096,128]{1,0:T(8,128)S(1)} custom-call(f32[2,2048,128]{2,1,0:T(8,128)S(1)} %bitcast.14, bf16[2,4,256,256]{3,2,1,0:T(8,128)(2,1)S(1)} %get-tuple-element.32.table_ref, f32[2,4,4,128,128]{4,3,2,1,0:T(8,128)S(1)} %get-tuple-element.33.twiddle_ref, f32[2,4,8,128]{3,2,1,0:T(8,128)S(1)} %get-tuple-element.34.turn_ref), custom_call_target="tpu_custom_call" | custom-call | flops 1610612736 | bytes 4194304 | tf_op jit(solution)/shard_map/pallas_call | solution.py:354
  5.5 0.0 copy-start.1
  5.5 67.8 %all_to_all.14 = f32[256,16,128]{2,1,0:T(8,128)S(1)} all-to-all(f32[256,16,128]{2,1,0:T(8,128)S(1)} %bitcast.10), channel_id=1, replica_groups=mesh['inner'=32,'outer'=8] {'inner','outer'}, dimensions={0} | all-to-all | bytes 4194304 | tf_op jit(solution)/shard_map/all_to_all | solution.py:424
  73.3 0.0 copy-done.1
  73.3 1.3 %shard_map.62 = f32[2304,128]{1,0:T(8,128)S(1)} custom-call(f32[4096,128]{1,0:T(8,128)S(1)} %bitcast.11, bf16[2,2,128,256]{3,2,1,0:T(8,128)(2,1)S(1)} %copy-done.1), custom_call_target="tpu_custom_call" | custom-call | flops 805306368 | bytes 4194304 | tf_op jit(solution)/shard_map/pallas_call | solution.py:367
  74.6 40.8 %all_to_all.15 = f32[256,1152,1]{1,2,0:T(1,128)S(1)} all-to-all(f32[256,1152,1]{1,2,0:T(1,128)S(1)} %bitcast.12), channel_id=1, replica_groups=mesh['inner'=32,'outer'=8] {'inner','outer'}, dimensions={0} | all-to-all | bytes 2359296 | tf_op jit(solution)/shard_map/all_to_all | solution.py:426
  115.4 3.0 %shard_map.63 = (f32[2048,128]{1,0:T(8,128)}, f32[256,128]{1,0:T(8,128)}) custom-call(s32[1]{0:T(128)} %bitcast.place_ref, f32[2304,128]{1,0:T(8,128)S(1)} %bitcast.13, s32[2,128,128]{2,1,0:T(8,128)S(1)} %get-tuple-element.35.code_ref, f32[5,2,128,128]{3,2,1,0:T(8,128)S(1)} %get-tuple-element.36.share_ref, f32[13,8,128]{2,1,0:T(8,128)S(1)} %get-tuple-element.37.entry_ref), custom_call_target="tpu_custom_call" | custom-call | flops 16777216 | bytes 4194304 | tf_op jit(solution)/shard_map/pallas_call | solution.py:392
Async XLA Ops:
  0.6 0.9 copy-start.2
  0.6 1.0 copy-start.3
  0.7 1.7 %copy-start = (f32[2,1,262144]{2,1,0:T(1,128)S(1)}, f32[2,1,262144]{2,1,0:T(1,128)}, u32[]{:S(2)}) copy-start(f32[2,1,262144]{2,1,0:T(1,128)} %param.4) | copy-start | bytes 6291460
  5.5 67.8 %copy-start.1 = (bf16[2,2,128,256]{3,2,1,0:T(8,128)(2,1)S(1)}, bf16[2,2,128,256]{3,2,1,0:T(8,128)(2,1)}, u32[]{:S(2)}) copy-start(bf16[2,2,128,256]{3,2,1,0:T(8,128)(2,1)} %constant.13.clone.table_ref) | copy-start | bytes 786436
